TPU v7x, 32 devices: a whole 2x2x4 slice. The times are simulated.
32 devices in a mesh: pipe: 2 (over x), dp: 16 (over z, y, core).
Axes of the slice: x: 2, y: 2, z: 4, core: 2. Of those that a mesh axis runs over, the one named last changes fastest.
Arguments:
- section_input: bfloat16 [2, 64, 512, 512], P('pipe', 'dp'), may hold values from -6 to 6
- attention_in: float32 [2, 512, 1536], P('pipe', 'dp'), may hold values from -0.25 to 0.25
- attention_out: float32 [2, 512, 512], P('pipe', 'dp'), may hold values from -1 to 1
- cross_weights: float32 [2, 512, 1024], P('pipe', 'dp')
- expand: float32 [2, 512, 2048], P('pipe', 'dp'), may hold values from -0.25 to 0.25
- contract: float32 [2, 2048, 512], P('pipe', 'dp'), may hold values from -0.125 to 0.125
- norm_gains: float32 [2, 3, 512], P('pipe', None, 'dp'), may hold values from 0.5 to 1.5
- source_lengths: int32 [64, 4], P('dp'), may hold values from 1 to 256, 512 in all within a row
- target_lengths: int32 [64, 4], P('dp'), may hold values from 1 to 256, 512 in all within a row
- cotangent: bfloat16 [64, 512, 512], P('dp'), may hold values from -6 to 6
Outputs:
- section_output: float32 [2, 64, 512, 512], P('pipe', 'dp')
- input_gradient: float32 [2, 64, 512, 512], P('pipe', 'dp')
- attention_in_gradient: float32 [2, 512, 1536], P('pipe', 'dp')
- attention_out_gradient: float32 [2, 512, 512], P('pipe', 'dp')
- cross_gradient: float32 [2, 512, 1024], P('pipe', 'dp')
- expand_gradient: float32 [2, 512, 2048], P('pipe', 'dp')
- contract_gradient: float32 [2, 2048, 512], P('pipe', 'dp')
- gains_gradient: float32 [2, 3, 512], P('pipe', None, 'dp')
All inputs are finite; a program needn't handle non-finite values.
Results may differ from a plain program's by a relative error of at most 0.018.
Values may be sent and summed in bfloat16 or wider, within the bound.
A program may use at most 256 MiB of HBM per device.

v0:
```python
from functools import partial

import jax
import jax.numpy as jnp
from jax import lax
from jax.sharding import PartitionSpec as P

D = 512
HEADS = 8
HD = 64
ROW = 512


EPSILON = 1e-05
MASKED = -1e30


def from_behind(value, axis, steps):
    count = lax.axis_size(axis)
    pairs = [(source, (source + steps) % count) for source in range(count)]
    return lax.ppermute(value, axis, pairs)


def matmul(left, right):
    return jnp.dot(left, right, preferred_element_type=jnp.float32)


def matmul_left(left, right):
    return lax.dot_general(
        left, right, (((0,), (0,)), ((), ())), preferred_element_type=jnp.float32
    )


def matmul_right(left, right):
    return lax.dot_general(
        left, right, (((1,), (1,)), ((), ())), preferred_element_type=jnp.float32
    )


def layer_norm(stream, gain):
    centre = jnp.mean(stream, axis=-1, keepdims=True)
    centred = stream - centre
    spread = jnp.mean(centred * centred, axis=-1, keepdims=True)
    return centred * lax.rsqrt(spread + EPSILON) * gain


def norm_back(stream, gain, delta):
    _, pull = jax.vjp(layer_norm, stream, gain)
    return pull(delta)


def segment_ids(lengths):
    ends = jnp.cumsum(lengths)
    places = jnp.arange(ROW, dtype=jnp.int32)
    return jnp.sum((places[:, None] >= ends[None, :]).astype(jnp.int32), axis=1)


def make_masks(source_count, target_count):
    source_seg = segment_ids(source_count)
    target_seg = segment_ids(target_count)
    places = jnp.arange(ROW, dtype=jnp.int32)
    encoder_mask = source_seg[:, None] == source_seg[None, :]
    decoder_mask = (target_seg[:, None] == target_seg[None, :]) & (
        places[None, :] <= places[:, None]
    )
    cross_mask = target_seg[:, None] == source_seg[None, :]
    return (encoder_mask, decoder_mask, cross_mask)


def split_heads(values):
    return values.reshape(values.shape[0], HEADS, HD)


def scores_of(query, keys, mask):
    raw = jnp.einsum(
        "qhd,khd->hqk", split_heads(query), split_heads(keys), preferred_element_type=jnp.float32
    ) * HD ** (-0.5)
    return jnp.where(mask[None], raw, MASKED)


def attend(query, keys, values, mask):
    scores = scores_of(query, keys, mask)
    top = jnp.max(scores, axis=-1, keepdims=True)
    weights = jnp.exp(scores - top)
    total = jnp.sum(weights, axis=-1, keepdims=True)
    shares = (weights / total).astype(jnp.bfloat16)
    result = jnp.einsum(
        "hqk,khd->qhd", shares, split_heads(values), preferred_element_type=jnp.float32
    )
    return (result.reshape(query.shape[0], D).astype(jnp.bfloat16), top + jnp.log(total))


def attend_back(query, keys, values, mask, logsum, delta_result):
    scores = scores_of(query, keys, mask)
    shares = jnp.exp(scores - logsum)
    delta_heads = split_heads(delta_result)
    delta_shares = jnp.einsum(
        "qhd,khd->hqk", delta_heads, split_heads(values), preferred_element_type=jnp.float32
    )
    delta_scores = shares * (delta_shares - jnp.sum(shares * delta_shares, axis=-1, keepdims=True))
    delta_low = delta_scores.astype(jnp.bfloat16)
    scale = HD ** (-0.5)
    delta_query = (
        jnp.einsum("hqk,khd->qhd", delta_low, split_heads(keys), preferred_element_type=jnp.float32)
        * scale
    )
    delta_keys = (
        jnp.einsum(
            "hqk,qhd->khd", delta_low, split_heads(query), preferred_element_type=jnp.float32
        )
        * scale
    )
    delta_values = jnp.einsum(
        "hqk,qhd->khd", shares.astype(jnp.bfloat16), delta_heads, preferred_element_type=jnp.float32
    )
    count = query.shape[0]
    return (
        delta_query.reshape(count, D),
        delta_keys.reshape(keys.shape[0], D),
        delta_values.reshape(values.shape[0], D),
    )


def self_block(stream, gain, project_in, project_out, mask):
    normed = layer_norm(stream, gain).astype(jnp.bfloat16)
    triple = matmul(normed, project_in).astype(jnp.bfloat16)
    result, logsum = attend(triple[:, :D], triple[:, D : 2 * D], triple[:, 2 * D :], mask)
    return (stream + matmul(result, project_out), (normed, triple, result, logsum))


def self_block_back(stream, gain, project_in, project_out, mask, kept, delta_out):
    normed, triple, result, logsum = kept
    delta_low = delta_out.astype(jnp.bfloat16)
    grad_out = matmul_left(result, delta_low)
    delta_result = matmul_right(delta_low, project_out).astype(jnp.bfloat16)
    parts = attend_back(
        triple[:, :D], triple[:, D : 2 * D], triple[:, 2 * D :], mask, logsum, delta_result
    )
    delta_triple = jnp.concatenate(parts, axis=1).astype(jnp.bfloat16)
    grad_in = matmul_left(normed, delta_triple)
    delta_normed = matmul_right(delta_triple, project_in)
    delta_stream, grad_gain = norm_back(stream, gain, delta_normed)
    return (delta_out + delta_stream, grad_gain, grad_in, grad_out)


def feed_block(stream, gain, expand, contract):
    normed = layer_norm(stream, gain).astype(jnp.bfloat16)
    hidden = matmul(normed, expand)
    active = jax.nn.gelu(hidden, approximate=False).astype(jnp.bfloat16)
    return (stream + matmul(active, contract), (normed, hidden, active))


def feed_block_back(stream, gain, expand, contract, kept, delta_out):
    normed, hidden, active = kept
    delta_low = delta_out.astype(jnp.bfloat16)
    grad_contract = matmul_left(active, delta_low)
    delta_active = matmul_right(delta_low, contract)
    _, pull = jax.vjp(lambda value: jax.nn.gelu(value, approximate=False), hidden)
    delta_hidden = pull(delta_active)[0].astype(jnp.bfloat16)
    grad_expand = matmul_left(normed, delta_hidden)
    delta_normed = matmul_right(delta_hidden, expand)
    delta_stream, grad_gain = norm_back(stream, gain, delta_normed)
    return (delta_out + delta_stream, grad_gain, grad_expand, grad_contract)


def cross_block(stream, gain, cross_pair, memory_pair, mask):
    normed = layer_norm(stream, gain).astype(jnp.bfloat16)
    question = matmul(normed, cross_pair[:, :D]).astype(jnp.bfloat16)
    result, logsum = attend(question, memory_pair[:, :D], memory_pair[:, D:], mask)
    return (stream + matmul(result, cross_pair[:, D:]), (normed, question, result, logsum))


def cross_block_back(stream, gain, cross_pair, memory_pair, mask, kept, delta_out):
    normed, question, result, logsum = kept
    delta_low = delta_out.astype(jnp.bfloat16)
    grad_output_part = matmul_left(result, delta_low)
    delta_result = matmul_right(delta_low, cross_pair[:, D:]).astype(jnp.bfloat16)
    delta_question, delta_keys, delta_values = attend_back(
        question, memory_pair[:, :D], memory_pair[:, D:], mask, logsum, delta_result
    )
    delta_question = delta_question.astype(jnp.bfloat16)
    grad_query_part = matmul_left(normed, delta_question)
    delta_normed = matmul_right(delta_question, cross_pair[:, :D])
    delta_stream, grad_gain = norm_back(stream, gain, delta_normed)
    delta_pair = jnp.concatenate([delta_keys, delta_values], axis=1).astype(jnp.bfloat16)
    grad_cross = jnp.concatenate([grad_query_part, grad_output_part], axis=1)
    return (delta_out + delta_stream, grad_gain, grad_cross, delta_pair)


def encoder_forward(stream, weights, mask):
    project_in, project_out, cross_pair, expand, contract, gains = weights
    first, kept_self = self_block(stream, gains[0], project_in, project_out, mask)
    second, kept_feed = feed_block(first, gains[1], expand, contract)
    memory = layer_norm(second, gains[2])
    memory_low = memory.astype(jnp.bfloat16)
    memory_pair = matmul(memory_low, cross_pair).astype(jnp.bfloat16)
    return (memory, memory_pair, (first, second, memory_low, kept_self, kept_feed))


def encoder_backward(stream, weights, mask, delta_pair):
    project_in, project_out, cross_pair, expand, contract, gains = weights
    _, _, kept = encoder_forward(stream, weights, mask)
    first, second, memory_low, kept_self, kept_feed = kept
    grad_cross = matmul_left(memory_low, delta_pair)
    delta_memory = matmul_right(delta_pair, cross_pair)
    delta_second, gain_last = norm_back(second, gains[2], delta_memory)
    delta_first, gain_feed, grad_expand, grad_contract = feed_block_back(
        first, gains[1], expand, contract, kept_feed, delta_second
    )
    delta_input, gain_self, grad_in, grad_out = self_block_back(
        stream, gains[0], project_in, project_out, mask, kept_self, delta_first
    )
    gain_grads = jnp.stack([gain_self, gain_feed, gain_last])
    return (delta_input, (grad_in, grad_out, grad_cross, grad_expand, grad_contract, gain_grads))


def decoder_pass(stream, memory_pair, weights, self_mask, cross_mask, delta_top):
    project_in, project_out, cross_pair, expand, contract, gains = weights
    first, kept_self = self_block(stream, gains[0], project_in, project_out, self_mask)
    second, kept_cross = cross_block(first, gains[1], cross_pair, memory_pair, cross_mask)
    third, kept_feed = feed_block(second, gains[2], expand, contract)
    delta_second, gain_feed, grad_expand, grad_contract = feed_block_back(
        second, gains[2], expand, contract, kept_feed, delta_top
    )
    delta_first, gain_cross, grad_cross, delta_pair = cross_block_back(
        first, gains[1], cross_pair, memory_pair, cross_mask, kept_cross, delta_second
    )
    delta_input, gain_self, grad_in, grad_out = self_block_back(
        stream, gains[0], project_in, project_out, self_mask, kept_self, delta_first
    )
    gain_grads = jnp.stack([gain_self, gain_cross, gain_feed])
    return (
        third,
        delta_input,
        delta_pair,
        (grad_in, grad_out, grad_cross, grad_expand, grad_contract, gain_grads),
    )


def add_terms(left, right):
    return tuple((first + second for first, second in zip(left, right)))


def encoder_work(turn, context, state):
    weights, rows, source_lengths, target_lengths, cotangent = context
    totals, outputs, gradients, received = state
    outgoing = jnp.zeros((rows.shape[1], 2 * D), jnp.bfloat16)
    count = rows.shape[0]
    if turn < count:
        encoder_mask, _, _ = make_masks(source_lengths[turn], target_lengths[turn])
        memory, outgoing, _ = encoder_forward(rows[turn].astype(jnp.float32), weights, encoder_mask)
        outputs = outputs.at[turn].set(memory)
    if turn >= 2:
        batch = turn - 2
        encoder_mask, _, _ = make_masks(source_lengths[batch], target_lengths[batch])
        delta_input, terms = encoder_backward(
            rows[batch].astype(jnp.float32), weights, encoder_mask, received
        )
        gradients = gradients.at[batch].set(delta_input)
        totals = add_terms(totals, terms)
    return (outgoing, totals, outputs, gradients)


def decoder_work(turn, context, state):
    weights, rows, source_lengths, target_lengths, cotangent = context
    totals, outputs, gradients, received = state
    outgoing = jnp.zeros((rows.shape[1], 2 * D), jnp.bfloat16)
    count = rows.shape[0]
    if 1 <= turn <= count:
        batch = turn - 1
        _, decoder_mask, cross_mask = make_masks(source_lengths[batch], target_lengths[batch])
        result, delta_input, outgoing, terms = decoder_pass(
            rows[batch].astype(jnp.float32),
            received,
            weights,
            decoder_mask,
            cross_mask,
            cotangent[batch].astype(jnp.float32),
        )
        outputs = outputs.at[batch].set(result)
        gradients = gradients.at[batch].set(delta_input)
        totals = add_terms(totals, terms)
    return (outgoing, totals, outputs, gradients)


def local(
    section_input,
    attention_in,
    attention_out,
    cross_weights,
    expand,
    contract,
    norm_gains,
    source_lengths,
    target_lengths,
    cotangent,
):
    section = lax.axis_index("pipe")
    gathered = (
        lax.all_gather(attention_in[0].astype(jnp.bfloat16), "dp", axis=0, tiled=True),
        lax.all_gather(attention_out[0].astype(jnp.bfloat16), "dp", axis=0, tiled=True),
        lax.all_gather(cross_weights[0].astype(jnp.bfloat16), "dp", axis=0, tiled=True),
        lax.all_gather(expand[0].astype(jnp.bfloat16), "dp", axis=0, tiled=True),
        lax.all_gather(contract[0].astype(jnp.bfloat16), "dp", axis=0, tiled=True),
        lax.all_gather(norm_gains[0].astype(jnp.bfloat16), "dp", axis=1, tiled=True),
    )
    weights = (
        gathered[0],
        gathered[1],
        gathered[2],
        gathered[3],
        gathered[4],
        gathered[5].astype(jnp.float32),
    )
    rows = section_input[0]
    count = rows.shape[0]
    context = (weights, rows, source_lengths, target_lengths, cotangent)
    zero_terms = tuple((jnp.zeros(weight.shape, jnp.float32) for weight in weights))
    totals = zero_terms
    shard_totals = None
    outputs = jnp.zeros(rows.shape, jnp.float32)
    gradients = jnp.zeros(rows.shape, jnp.float32)
    received = jnp.zeros((rows.shape[1], 2 * D), jnp.bfloat16)
    for turn in range(count + 2):
        outgoing, totals, outputs, gradients = lax.cond(
            section == 0,
            partial(encoder_work, turn, context),
            partial(decoder_work, turn, context),
            (totals, outputs, gradients, received),
        )
        if turn <= count:
            received = from_behind(outgoing, "pipe", 1)
    shard_totals = (
        lax.psum_scatter(totals[0], "dp", scatter_dimension=0, tiled=True),
        lax.psum_scatter(totals[1], "dp", scatter_dimension=0, tiled=True),
        lax.psum_scatter(totals[2], "dp", scatter_dimension=0, tiled=True),
        lax.psum_scatter(totals[3], "dp", scatter_dimension=0, tiled=True),
        lax.psum_scatter(totals[4], "dp", scatter_dimension=0, tiled=True),
        lax.psum_scatter(totals[5], "dp", scatter_dimension=1, tiled=True),
    )
    return (
        outputs[None],
        gradients[None],
        shard_totals[0][None],
        shard_totals[1][None],
        shard_totals[2][None],
        shard_totals[3][None],
        shard_totals[4][None],
        shard_totals[5][None],
    )


def solution(mesh):
    in_specs = (
        P("pipe", "dp", None, None),
        P("pipe", "dp", None),
        P("pipe", "dp", None),
        P("pipe", "dp", None),
        P("pipe", "dp", None),
        P("pipe", "dp", None),
        P("pipe", None, "dp"),
        P("dp", None),
        P("dp", None),
        P("dp", None, None),
    )
    out_specs = (
        P("pipe", "dp", None, None),
        P("pipe", "dp", None, None),
        P("pipe", "dp", None),
        P("pipe", "dp", None),
        P("pipe", "dp", None),
        P("pipe", "dp", None),
        P("pipe", "dp", None),
        P("pipe", None, "dp"),
    )
    return jax.shard_map(local, mesh=mesh, in_specs=in_specs, out_specs=out_specs, check_vma=False)
```

profile of v0, /device:TPU:0, one launch (start us, length us, event | category | flops | bytes accessed | tf_op | source)
XLA Modules:
  0.0 1408.0 jit_solution(16813317013840111453)
XLA Ops:
  16.8 24.0 %all-gather = bf16[1,3,512]{1,0,2:T(2,128)(2,1)S(1)} all-gather(bf16[1,3,32]{1,0,2:T(2,128)(2,1)S(1)} %copy.644), channel_id=2, replica_groups=mesh['pipe'=2,'dp'=16] {'dp'}, dimensions={2}, use_global_device_ids=true | all-gather | bytes 3264 | tf_op jit(solution)/shard_map/all_gather | solution.py:305
  41.2 19.4 %all-gather.2 = bf16[1,512,512]{2,1,0:T(8,128)(2,1)S(1)} all-gather(bf16[1,32,512]{2,1,0:T(8,128)(2,1)S(1)} %convert_element_type.816), channel_id=4, replica_groups=mesh['pipe'=2,'dp'=16] {'dp'}, dimensions={1}, use_global_device_ids=true | all-gather | bytes 557056 | tf_op jit(solution)/shard_map/all_gather | solution.py:301
  60.5 33.2 %all-gather.11.cloned.1.call-done = bf16[1,512,1536]{2,1,0:T(8,128)(2,1)} async-done(((bf16[1,32,1536]{2,1,0:T(8,128)(2,1)}), bf16[1,512,1536]{2,1,0:T(8,128)(2,1)}) %all-gather.11.cloned.1.call-update) | async-done | bytes 1572880 | tf_op jit(solution)/shard_map/all_gather | solution.py:300
  93.7 43.1 %all-gather.15.cloned.1.call-done = bf16[1,512,2048]{2,1,0:T(8,128)(2,1)} async-done(((bf16[1,32,2048]{2,1,0:T(8,128)(2,1)}), bf16[1,512,2048]{2,1,0:T(8,128)(2,1)}) %all-gather.15.cloned.1.call-update) | async-done | bytes 2097168 | tf_op jit(solution)/shard_map/all_gather | solution.py:303
  136.8 42.8 %all-gather.17.cloned.1.call-done = bf16[1,2048,512]{2,1,0:T(8,128)(2,1)} async-done(((bf16[1,128,512]{2,1,0:T(8,128)(2,1)}), bf16[1,2048,512]{2,1,0:T(8,128)(2,1)}) %all-gather.17.cloned.1.call-update) | async-done | bytes 2097168 | tf_op jit(solution)/shard_map/all_gather | solution.py:304
  179.6 46.8 %conditional.9 = (bf16[512,1024]{1,0:T(8,128)(2,1)}, f32[4,512,512]{1,2,0:T(8,128)}) conditional(s32[]{:T(128)} %convert_element_type.810, () %tuple.133, (bf16[4,512,512]{1,2,0:T(8,128)(2,1)S(1)}, f32[3,512]{0,1:T(8,128)S(1)}, bf16[512,1536]{1,0:T(8,128)(2,1)}, s32[4,4]{1,0:T(4,128)S(1)}, bf16[512,512]{1,0:T(8,128)(2,1)S(1)}, ...), branch_computations={%region_0.0_spmd, %region_1.12_spmd} | conditional | flops 4386201088 | bytes 62519484 | solution.py:325
  189.9 7.7 fusion.769
  197.6 4.2 fusion.22
  203.5 15.1 %fusion.771 = (f32[512]{0:T(512)S(1)}, f32[512,512]{0,1:T(8,128)}) fusion(f32[512,512]{0,1:T(8,128)} %copy-done.125, bf16[2048,512]{1,0:T(8,128)(2,1)} %get-tuple-element.557, bf16[512,2048]{1,0:T(8,128)(2,1)} %get-tuple-element.556, f32[512]{0:T(512)S(1)} %bitcast.1462, f32[512]{0:T(512)S(1)} %add_rsqrt_fusion.1, f32[512]{0:T(512)S(1)} %broadcast_multiply_fusion.1), kind=kOutput, calls=%fused_computation.1378 | convolution fusion | flops 2217213440 | bytes 6299648 | tf_op jit(solution)/shard_map/cond/branch_1_fun/dot_general | solution.py:25
  220.2 3.4 convolution_convert_fusion.1
  228.7 25.6 %collective-permute-done = bf16[512,1024]{0,1:T(8,128)(2,1)} collective-permute-done((bf16[512,1024]{0,1:T(8,128)(2,1)}, bf16[512,1024]{0,1:T(8,128)(2,1)}, u32[]{:S(2)}, u32[]{:S(2)}) %collective-permute-start) | collective-permute-done | bytes 1048608 | tf_op jit(solution)/shard_map/ppermute | solution.py:21
  254.3 67.6 %conditional.10 = (bf16[512,1024]{0,1:T(8,128)(2,1)}, f32[512,1536]{1,0:T(8,128)}, f32[512,512]{1,0:T(8,128)}, f32[512,1024]{0,1:T(8,128)}, f32[512,2048]{1,0:T(...) conditional(s32[]{:T(128)} %convert_element_type.810, ...), branch_computations={%region_12.38_spmd, %region_38.49_spmd} | conditional | flops 14697111552 | bytes 542254400
  273.5 7.7 fusion.774
  281.2 4.2 fusion.167
  289.7 16.4 %fusion.776 = (f32[512]{0:T(512)S(1)}, f32[512,512]{0,1:T(8,128)}) fusion(f32[512,512]{0,1:T(8,128)} %copy-done.124, bf16[2048,512]{1,0:T(8,128)(2,1)} %get-tuple-element.577, f32[512,2048]{1,0:T(8,128)} %broadcast.2435, bf16[512,2048]{1,0:T(8,128)(2,1)} %get-tuple-element.576, f32[512]{0:T(512)S(1)} %bitcast.1461, f32[512]{0:T(512)S(1)} %add_rsqrt_fusion.4, ...), kind=kOutput, calls=%fused_computation.1383 | convolution fusion | flops 2217213440 | bytes 10493952 | tf_op jit(solution)/shard_map/cond/branch_1_fun/dot_general | solution.py:25
  307.5 3.3 fusion.176
  324.3 47.8 %collective-permute-start.1 = (bf16[512,1024]{1,0:T(8,128)(2,1)}, bf16[512,1024]{1,0:T(8,128)(2,1)}, u32[]{:S(2)}, u32[]{:S(2)}) collective-permute-start(bf16[512,1024]{1,0:T(8,128)(2,1)} %copy.650), channel_id=1, source_target_pairs={{0,16},{16,0},{1,17},{17,1},{2,18},{18,2},{3,19},{19,3},{4,20},{20... | collective-permute-start | bytes 3145736 | tf_op jit(solution)/shard_map/ppermute | solution.py:21
  372.0 23.4 %collective-permute-done.1 = bf16[512,1024]{1,0:T(8,128)(2,1)} collective-permute-done((bf16[512,1024]{1,0:T(8,128)(2,1)}, bf16[512,1024]{1,0:T(8,128)(2,1)}, u32[]{:S(2)}, u32[]{:S(2)}) %collective-permute-start.1) | collective-permute-done | bytes 1048608 | tf_op jit(solution)/shard_map/ppermute | solution.py:21
  395.4 126.6 %conditional.11 = (bf16[512,1024]{1,0:T(8,128)(2,1)}, f32[512,1536]{1,0:T(8,128)}, f32[512,512]{1,0:T(8,128)}, f32[512,1024]{1,0:T(8,128)}, f32[512,2048]{1,0:T(...) conditional(s32[]{:T(128)} %convert_element_type.810, ...), branch_computations={%region_49.75_spmd, %region_75.106_spmd} | conditional | flops 16895198208 | bytes 571620800
  419.3 10.4 multiply_convert_fusion.31
  459.6 7.6 fusion.797
  467.2 4.4 fusion.325
  473.4 15.2 %fusion.799 = (f32[512]{0:T(512)S(1)}, f32[512,512]{0,1:T(8,128)}) fusion(f32[512,512]{0,1:T(8,128)} %copy-done.126, bf16[2048,512]{1,0:T(8,128)(2,1)} %get-tuple-element.605, bf16[512,2048]{1,0:T(8,128)(2,1)} %get-tuple-element.604, f32[512]{0:T(512)S(1)} %bitcast.1370, f32[512]{0:T(512)S(1)} %add_rsqrt_fusion.7, f32[512]{0:T(512)S(1)} %broadcast_multiply_fusion.16), kind=kOutput, calls=%fused_computation.1406 | convolution fusion | flops 2217213440 | bytes 6299648 | tf_op jit(solution)/shard_map/cond/branch_1_fun/dot_general | solution.py:25
  490.0 3.5 fusion.346
  493.5 4.7 convolution_add_fusion.12
  503.8 4.5 convolution_add_fusion.15
  508.3 5.7 convolution_add_fusion.14
  514.0 5.7 convolution_add_fusion.13
  522.0 30.0 %collective-permute-start.2 = (bf16[512,1024]{1,0:T(8,128)(2,1)}, bf16[512,1024]{1,0:T(8,128)(2,1)}, u32[]{:S(2)}, u32[]{:S(2)}) collective-permute-start(bf16[512,1024]{1,0:T(8,128)(2,1)} %get-tuple-element.775), channel_id=1, source_target_pairs={{0,16},{16,0},{1,17},{17,1},{2,18},{18,2},{3,19},{19,3},{4,20},{20... | collective-permute-start | bytes 3145736 | tf_op jit(solution)/shard_map/ppermute | solution.py:21
  552.0 22.5 %collective-permute-done.2 = bf16[512,1024]{1,0:T(8,128)(2,1)} collective-permute-done((bf16[512,1024]{1,0:T(8,128)(2,1)}, bf16[512,1024]{1,0:T(8,128)(2,1)}, u32[]{:S(2)}, u32[]{:S(2)}) %collective-permute-start.2) | collective-permute-done | bytes 1048608 | tf_op jit(solution)/shard_map/ppermute | solution.py:21
  574.5 123.1 %conditional.12 = (bf16[512,1024]{1,0:T(8,128)(2,1)}, f32[512,1536]{1,0:T(8,128)}, f32[512,512]{1,0:T(8,128)}, f32[512,1024]{1,0:T(8,128)}, f32[512,2048]{1,0:T(...) conditional(s32[]{:T(128)} %convert_element_type.810, ...), branch_computations={%region_106.132_spmd, %region_132.163_spmd} | conditional | flops 16895198208 | bytes 588397888
  598.1 10.5 multiply_convert_fusion.53
  638.4 7.6 fusion.813
  646.1 4.4 fusion.510
  652.1 15.2 %fusion.815 = (f32[512]{0:T(512)S(1)}, f32[512,512]{0,1:T(8,128)}) fusion(f32[512,512]{0,1:T(8,128)} %copy-done.127, bf16[2048,512]{1,0:T(8,128)(2,1)} %get-tuple-element.641, bf16[512,2048]{1,0:T(8,128)(2,1)} %get-tuple-element.640, f32[512]{0:T(512)S(1)} %bitcast.1375, f32[512]{0:T(512)S(1)} %add_rsqrt_fusion.10, f32[512]{0:T(512)S(1)} %broadcast_multiply_fusion.25), kind=kOutput, calls=%fused_computation.1422 | convolution fusion | flops 2217213440 | bytes 6299648 | tf_op jit(solution)/shard_map/cond/branch_1_fun/dot_general | solution.py:25
  668.9 3.4 fusion.531
  672.3 4.7 convolution_add_fusion.27
  679.8 4.1 convolution_add_fusion.30
  683.9 5.7 convolution_add_fusion.29
  689.6 5.7 convolution_add_fusion.28
  697.6 37.3 %collective-permute-start.3 = (bf16[512,1024]{1,0:T(8,128)(2,1)}, bf16[512,1024]{1,0:T(8,128)(2,1)}, u32[]{:S(2)}, u32[]{:S(2)}) collective-permute-start(bf16[512,1024]{1,0:T(8,128)(2,1)} %get-tuple-element.784), channel_id=1, source_target_pairs={{0,16},{16,0},{1,17},{17,1},{2,18},{18,2},{3,19},{19,3},{4,20},{20... | collective-permute-start | bytes 3145736 | tf_op jit(solution)/shard_map/ppermute | solution.py:21
  734.9 21.6 %collective-permute-done.3 = bf16[512,1024]{1,0:T(8,128)(2,1)} collective-permute-done((bf16[512,1024]{1,0:T(8,128)(2,1)}, bf16[512,1024]{1,0:T(8,128)(2,1)}, u32[]{:S(2)}, u32[]{:S(2)}) %collective-permute-start.3) | collective-permute-done | bytes 1048608 | tf_op jit(solution)/shard_map/ppermute | solution.py:21
  756.4 88.9 %conditional.13 = (bf16[512,1024]{0,1:T(8,128)(2,1)}, f32[512,1536]{1,0:T(8,128)}, f32[512,512]{1,0:T(8,128)}, f32[512,1024]{0,1:T(8,128)}, f32[512,2048]{1,0:T(...) conditional(s32[]{:T(128)} %convert_element_type.810, ...), branch_computations={%region_163.189_spmd, %region_189.210_spmd} | conditional | flops 14701044736 | bytes 607272320 | solution.py:325
  780.0 10.4 multiply_convert_fusion.75
  808.9 4.6 convolution_add_fusion.42
  816.3 4.0 convolution_add_fusion.45
  820.3 3.1 copy.634
  823.4 6.6 convolution_add_fusion.44
  830.0 5.7 convolution_add_fusion.43
  838.7 5.2 copy.733
  847.6 55.3 %collective-permute-start.4 = (bf16[512,1024]{1,0:T(8,128)(2,1)}, bf16[512,1024]{1,0:T(8,128)(2,1)}, u32[]{:S(2)}, u32[]{:S(2)}) collective-permute-start(bf16[512,1024]{1,0:T(8,128)(2,1)} %copy.666), channel_id=1, source_target_pairs={{0,16},{16,0},{1,17},{17,1},{2,18},{18,2},{3,19},{19,3},{4,20},{20... | collective-permute-start | bytes 3145736 | tf_op jit(solution)/shard_map/ppermute | solution.py:21
  902.9 20.6 %collective-permute-done.4 = bf16[512,1024]{1,0:T(8,128)(2,1)} collective-permute-done((bf16[512,1024]{1,0:T(8,128)(2,1)}, bf16[512,1024]{1,0:T(8,128)(2,1)}, u32[]{:S(2)}, u32[]{:S(2)}) %collective-permute-start.4) | collective-permute-done | bytes 1048608 | tf_op jit(solution)/shard_map/ppermute | solution.py:21
  923.5 74.5 %conditional.14 = (f32[512,1536]{1,0:T(8,128)}, f32[512,512]{1,0:T(8,128)}, f32[512,1024]{1,0:T(8,128)S(1)}, f32[512,2048]{1,0:T(8,128)}, f32[2048,512]{1,0:T(8,...) conditional(s32[]{:T(128)} %convert_element_type.810, (f32[4,512,512]{1,2,0:T(8,128)}, ...), branch_computations={%region_210.211_spmd, %region_211.232_spmd} | conditional | flops 12509522944 | bytes 391566240 | solution.py:325
  938.5 10.5 multiply_convert_fusion.82
  967.5 4.6 convolution_add_fusion.49
  978.0 4.4 convolution_add_fusion.52
  982.4 3.3 convolution_add_fusion.51
  992.4 5.4 copy.735
  1002.5 50.2 %reduce-scatter.19.cloned.1.call-done = f32[32,3]{1,0:T(8,128)} async-done(((f32[512,3]{1,0:T(8,128)}), f32[32,3]{1,0:T(8,128)}) %reduce-scatter.19.cloned.1.call-update) | async-done | bytes 400
  1054.0 59.1 %reduce-scatter.11.cloned.1.call-done = f32[32,512]{1,0:T(8,128)} async-done(((f32[512,512]{1,0:T(8,128)}), f32[32,512]{1,0:T(8,128)}) %reduce-scatter.11.cloned.1.call-update) | async-done | bytes 65552 | tf_op jit(solution)/shard_map/reduce_scatter | solution.py:335
  1113.1 65.5 %reduce-scatter.13.cloned.1.call-done = f32[32,1024]{1,0:T(8,128)} async-done(((f32[512,1024]{1,0:T(8,128)}), f32[32,1024]{1,0:T(8,128)}) %reduce-scatter.13.cloned.1.call-update) | async-done | bytes 131088 | tf_op jit(solution)/shard_map/reduce_scatter | solution.py:336
  1178.6 69.6 %reduce-scatter.9.cloned.1.call-done = f32[32,1536]{1,0:T(8,128)} async-done(((f32[512,1536]{1,0:T(8,128)}), f32[32,1536]{1,0:T(8,128)}) %reduce-scatter.9.cloned.1.call-update) | async-done | bytes 196624 | tf_op jit(solution)/shard_map/reduce_scatter | solution.py:334
  1248.2 76.1 %reduce-scatter.15.cloned.1.call-done = f32[32,2048]{1,0:T(8,128)} async-done(((f32[512,2048]{1,0:T(8,128)}), f32[32,2048]{1,0:T(8,128)}) %reduce-scatter.15.cloned.1.call-update) | async-done | bytes 262160 | tf_op jit(solution)/shard_map/reduce_scatter | solution.py:337
  1324.3 76.6 %reduce-scatter.17.cloned.1.call-done = f32[128,512]{1,0:T(8,128)} async-done(((f32[2048,512]{1,0:T(8,128)}), f32[128,512]{1,0:T(8,128)}) %reduce-scatter.17.cloned.1.call-update) | async-done | bytes 262160 | tf_op jit(solution)/shard_map/reduce_scatter | solution.py:338
  (553 shorter events, 258.6 us)
Async XLA Ops:
  7.2 9.6 copy-start.241
  7.2 34.0 %copy-start.239 = (f32[1,32,512]{2,1,0:T(8,128)S(1)}, f32[1,32,512]{2,1,0:T(8,128)}, u32[]{:S(2)}) copy-start(f32[1,32,512]{2,1,0:T(8,128)} %param.56) | copy-start | bytes 196612
  7.2 172.4 %copy-start.240 = (s32[4,4]{1,0:T(4,128)S(1)}, s32[4,4]{1,0:T(4,128)}, u32[]{:S(2)}) copy-start(s32[4,4]{1,0:T(4,128)} %param.61) | copy-start | bytes 196
  7.2 53.3 %all-gather.13.cloned.1.call-start = ((), (), s32[]{:S(2)}) async-start(), calls=%async_computation.12 | async-start | bytes 1114112 | tf_op jit(solution)/shard_map/all_gather | solution.py:302
  8.8 84.9 %all-gather.11.cloned.1.call-start = ((), (), s32[]{:S(2)}) async-start(), calls=%async_computation.11 | async-start | bytes 1671168 | tf_op jit(solution)/shard_map/all_gather | solution.py:300
  10.5 126.3 %all-gather.15.cloned.1.call-start = ((), (), s32[]{:S(2)}) async-start(), calls=%async_computation.13 | async-start | bytes 2228224 | tf_op jit(solution)/shard_map/all_gather | solution.py:303
  12.2 167.4 %all-gather.17.cloned.1.call-start = ((), (), s32[]{:S(2)}) async-start(), calls=%async_computation.14 | async-start | bytes 2228224 | tf_op jit(solution)/shard_map/all_gather | solution.py:304
  13.9 1038.8 %reduce-scatter.19.cloned.1.call-start = ((), (), s32[]{:S(2)}) async-start(), calls=%async_computation.15 | async-start | bytes 278528
  189.9 7.7 copy-start.237
  218.7 4.8 copy-start.123
  228.7 25.6 %collective-permute-start = (bf16[512,1024]{0,1:T(8,128)(2,1)}, bf16[512,1024]{0,1:T(8,128)(2,1)}, u32[]{:S(2)}, u32[]{:S(2)}) collective-permute-start(bf16[512,1024]{0,1:T(8,128)(2,1)} %copy.646), channel_id=1, source_target_pairs={{0,16},{16,0},{1,17},{17,1},{2,18},{18,2},{3,19},{19,3},{4,20},{20... | collective-permute-start | bytes 3145736 | tf_op jit(solution)/shard_map/ppermute | solution.py:21
  273.5 7.7 copy-start.238
  306.0 4.8 copy-start.122
  324.3 71.2 %collective-permute-start.1 = (bf16[512,1024]{1,0:T(8,128)(2,1)}, bf16[512,1024]{1,0:T(8,128)(2,1)}, u32[]{:S(2)}, u32[]{:S(2)}) collective-permute-start(bf16[512,1024]{1,0:T(8,128)(2,1)} %copy.650), channel_id=1, source_target_pairs={{0,16},{16,0},{1,17},{17,1},{2,18},{18,2},{3,19},{19,3},{4,20},{20... | collective-permute-start | bytes 3145736 | tf_op jit(solution)/shard_map/ppermute | solution.py:21
  418.5 11.2 copy-start.223
  419.0 19.4 %copy-start.22 = (f32[512,512]{0,1:T(8,128)}, f32[512,512]{0,1:T(8,128)S(1)}, u32[]{:S(2)}) copy-start(f32[512,512]{0,1:T(8,128)S(1)} %get-tuple-element.1921) | copy-start | bytes 3145732 | tf_op jit(solution)/shard_map/conditional.1
  419.2 10.5 copy-start.256
  441.0 7.2 copy-start.147
  488.5 4.9 copy-start.148
  488.5 4.9 copy-start.152
  508.2 5.7 copy-start.65
  508.3 5.7 copy-start.89
  514.0 5.7 copy-start.77
  514.0 5.7 copy-start.129
  514.0 5.7 copy-start.132
  522.0 52.5 %collective-permute-start.2 = (bf16[512,1024]{1,0:T(8,128)(2,1)}, bf16[512,1024]{1,0:T(8,128)(2,1)}, u32[]{:S(2)}, u32[]{:S(2)}) collective-permute-start(bf16[512,1024]{1,0:T(8,128)(2,1)} %get-tuple-element.775), channel_id=1, source_target_pairs={{0,16},{16,0},{1,17},{17,1},{2,18},{18,2},{3,19},{19,3},{4,20},{20... | collective-permute-start | bytes 3145736 | tf_op jit(solution)/shard_map/ppermute | solution.py:21
  597.4 11.2 copy-start.225
  597.9 19.5 %copy-start.24 = (f32[512,512]{0,1:T(8,128)}, f32[512,512]{0,1:T(8,128)S(1)}, u32[]{:S(2)}) copy-start(f32[512,512]{0,1:T(8,128)S(1)} %get-tuple-element.1983) | copy-start | bytes 3145732 | tf_op jit(solution)/shard_map/conditional.2
  598.1 10.5 copy-start.258
  619.9 7.2 copy-start.149
  667.4 4.8 copy-start.150
  667.4 4.8 copy-start.154
  672.2 4.7 copy-start.111
  672.2 7.6 copy-start.74
  677.0 6.9 copy-start.25
  677.0 6.9 copy-start.138
  683.9 5.7 copy-start.67
  683.9 5.7 copy-start.91
  689.6 5.8 copy-start.79
  689.6 5.8 copy-start.131
  689.6 5.8 copy-start.133
  697.6 58.8 %collective-permute-start.3 = (bf16[512,1024]{1,0:T(8,128)(2,1)}, bf16[512,1024]{1,0:T(8,128)(2,1)}, u32[]{:S(2)}, u32[]{:S(2)}) collective-permute-start(bf16[512,1024]{1,0:T(8,128)(2,1)} %get-tuple-element.784), channel_id=1, source_target_pairs={{0,16},{16,0},{1,17},{17,1},{2,18},{18,2},{3,19},{19,3},{4,20},{20... | collective-permute-start | bytes 3145736 | tf_op jit(solution)/shard_map/ppermute | solution.py:21
  779.8 19.6 %copy-start.28 = (f32[512,512]{0,1:T(8,128)}, f32[512,512]{0,1:T(8,128)S(1)}, u32[]{:S(2)}) copy-start(f32[512,512]{0,1:T(8,128)S(1)} %get-tuple-element.2040) | copy-start | bytes 3145732 | tf_op jit(solution)/shard_map/cond
  780.0 10.5 copy-start.260
  794.9 4.8 copy-start.62
  801.9 7.0 copy-start.171
  808.1 5.4 copy-start.185
  823.4 6.6 copy-start.63
  823.4 6.6 copy-start.95
  830.0 5.7 copy-start.172
  830.0 5.7 copy-start.186
  830.0 5.7 copy-start.268
  847.6 75.9 %collective-permute-start.4 = (bf16[512,1024]{1,0:T(8,128)(2,1)}, bf16[512,1024]{1,0:T(8,128)(2,1)}, u32[]{:S(2)}, u32[]{:S(2)}) collective-permute-start(bf16[512,1024]{1,0:T(8,128)(2,1)} %copy.666), channel_id=1, source_target_pairs={{0,16},{16,0},{1,17},{17,1},{2,18},{18,2},{3,19},{19,3},{4,20},{20... | collective-permute-start | bytes 3145736 | tf_op jit(solution)/shard_map/ppermute | solution.py:21
  938.3 19.7 %copy-start.26 = (f32[512,512]{0,1:T(8,128)}, f32[512,512]{0,1:T(8,128)S(1)}, u32[]{:S(2)}) copy-start(f32[512,512]{0,1:T(8,128)S(1)} %get-tuple-element.2059) | copy-start | bytes 3145732 | tf_op jit(solution)/shard_map/cond
  938.5 10.5 copy-start.261
  953.5 4.8 copy-start.60
  960.5 7.0 copy-start.169
  966.7 5.4 copy-start.183
  992.4 5.4 copy-start.86
  999.1 114.0 %reduce-scatter.11.cloned.1.call-start = ((), (), s32[]{:S(2)}) async-start(), calls=%async_computation.7 | async-start | bytes 1114112 | tf_op jit(solution)/shard_map/reduce_scatter | solution.py:335
  999.7 178.9 %reduce-scatter.13.cloned.1.call-start = ((), (), s32[]{:S(2)}) async-start(), calls=%async_computation.8 | async-start | bytes 2228224 | tf_op jit(solution)/shard_map/reduce_scatter | solution.py:336
  1000.4 247.7 %reduce-scatter.9.cloned.1.call-start = ((), (), s32[]{:S(2)}) async-start(), calls=%async_computation.6 | async-start | bytes 3342336 | tf_op jit(solution)/shard_map/reduce_scatter | solution.py:334
  1001.2 323.1 %reduce-scatter.15.cloned.1.call-start = ((), (), s32[]{:S(2)}) async-start(), calls=%async_computation.9 | async-start | bytes 4456448 | tf_op jit(solution)/shard_map/reduce_scatter | solution.py:337
  1001.9 399.0 %reduce-scatter.17.cloned.1.call-start = ((), (), s32[]{:S(2)}) async-start(), calls=%async_computation.10 | async-start | bytes 4456448 | tf_op jit(solution)/shard_map/reduce_scatter | solution.py:338
  (63 other events, 146.0 us)
Sparse Core Ops, SparseCore 0:
  10.8 41.3 all-gather.12
  55.1 38.6 all-gather.10
  96.5 40.2 all-gather.14
  139.4 40.1 all-gather.16
  999.2 53.3 reduce-scatter.18
  1056.7 56.3 reduce-scatter.10
  1117.9 60.6 reduce-scatter.12
  1183.0 65.1 reduce-scatter.8
  1252.6 71.6 reduce-scatter.14
  1329.1 71.8 reduce-scatter.16
where the time goes:
time: 1420 us; the launch traced here: 1410 us
  waiting for transfers between devices  633 us (45%)
  matrix products  350 us (25%)
  starting transfers between devices  171 us (12%)
  local copies, waits for them, and re-layouts  105 us (7%)
  other arithmetic  52.9 us (4%)
  blocking collectives  43.4 us (3%)
  loops' own time  38.5 us (3%)
  between operations  14.6 us (1%)
    ppermute x5, starting transfers between devices, from_behind(): return lax.ppermute(value, axis, pairs)  170 us
    dot_general x32, matrix products, matmul(): return jnp.dot(left, right, preferred_element_type=jnp.float32)  144 us
    ppermute x5, waiting for transfers between devices, from_behind(): return lax.ppermute(value, axis, pairs)  114 us
    dot_general x20, matrix products, matmul_left(): lax.dot_general(left, right, (((0,), (0,)), ((), ())), preferred_element_...  87 us
    reduce_scatter x1, waiting for transfers between devices, local(): lax.psum_scatter(totals[4], 'dp', scatter_dimension=0, tiled=True)  76.6 us
    reduce_scatter x1, waiting for transfers between devices, local(): lax.psum_scatter(totals[3], 'dp', scatter_dimension=0, tiled=True)  76.1 us
    reduce_scatter x1, waiting for transfers between devices, local(): lax.psum_scatter(totals[0], 'dp', scatter_dimension=0, tiled=True)  69.6 us
    reduce_scatter x1, waiting for transfers between devices, local(): lax.psum_scatter(totals[2], 'dp', scatter_dimension=0, tiled=True)  65.5 us
  transfers between devices with their start and end apart: 15, of which 14 were waited for; matrix products, arithmetic and copies ran while one was open for 1% of the time, Pallas kernels for 0%

commit v1 on v0

v1 whole, which is shorter than its diff:
```python
from functools import partial
import math

import jax
import jax.numpy as jnp
from jax import lax
from jax.experimental import pallas as pl
from jax.experimental.pallas import tpu as pltpu
from jax.sharding import PartitionSpec as P

D = 512
HEADS = 8
HD = 64
FF = 2048
ROW = 512
PAIRS = HEADS // 2
PACK = 4

QKV, OUT, CROSS, EXPAND, BLOCKS = 0, 3, 4, 6, 10
SLABS = FF // D

EPSILON = 1e-05
MASKED = -1e30
LOG2E = math.log2(math.e)
EXPONENT = HD**-0.5 * LOG2E
BELL = 1.0 / math.sqrt(2.0 * math.pi)
LOW = jnp.bfloat16
FULL = jnp.float32
VMEM_LIMIT = 62 * 2**20

NN = (((1,), (0,)), ((), ()))
NT = (((1,), (1,)), ((), ()))
TN = (((0,), (0,)), ((), ()))


def multiply(left, right, dims=NN):
    return lax.dot_general(left, right, dims, preferred_element_type=jnp.float32)


def columns(index, width=D):
    return pl.ds(index * width, width)


def normalize(stream):
    centred = stream - jnp.mean(stream, axis=1, keepdims=True)
    scale = lax.rsqrt(jnp.mean(centred * centred, axis=1, keepdims=True) + EPSILON)
    return centred * scale, scale


def norm_back(unit, scale, gain, delta):
    inner = delta * gain
    mean = jnp.mean(inner, axis=1, keepdims=True)
    along = jnp.mean(inner * unit, axis=1, keepdims=True)
    return scale * (inner - mean - unit * along), jnp.sum(delta * unit, axis=0, keepdims=True)


def segment(counts, row, shape, axis):
    places = lax.broadcasted_iota(jnp.int32, shape, axis)
    end = counts[row, 0]
    found = (places >= end).astype(jnp.int32)
    for piece in range(1, PACK):
        end = end + counts[row, piece]
        found = found + (places >= end).astype(jnp.int32)
    return found


def fill_bias(bias, query_counts, key_counts, row, causal):
    keep = segment(query_counts, row, (ROW, 1), 0) == segment(key_counts, row, (1, ROW), 1)
    if causal:
        query = lax.broadcasted_iota(jnp.int32, (ROW, ROW), 0)
        key = lax.broadcasted_iota(jnp.int32, (ROW, ROW), 1)
        keep = keep & (key <= query)
    bias[...] = jnp.where(keep, 0.0, MASKED)


def lanes():
    return lax.broadcasted_iota(jnp.int32, (1, 2 * HD), 1)


def only_half(value, half):
    return jnp.where(lanes() // HD == half, value, jnp.zeros_like(value))


def attend(query, keys, values, bias, shares, inverse, result):
    kept = jnp.zeros((ROW, 2 * HD), FULL)
    for pair in range(PAIRS):
        query2, keys2, values2 = query(pair), keys(pair), values(pair)
        parts = []
        for half in range(2):
            head = 2 * pair + half
            scores = multiply(only_half(query2, half), keys2, NT) + bias[...]
            top = jnp.max(scores, axis=1, keepdims=True)
            weights = jnp.exp2((scores - top) * EXPONENT)
            scale = 1.0 / jnp.sum(weights, axis=1, keepdims=True)
            low = weights.astype(LOW)
            shares[head] = low
            parts.append(multiply(low, values2) * scale)
            kept = jnp.where(lanes() == head, scale, kept)
        result[:, columns(pair, 2 * HD)] = jnp.where(lanes() < HD, parts[0], parts[1]).astype(LOW)
    inverse[...] = kept


def attend_back(query, keys, values, shares, inverse, result, delta, put):
    for pair in range(PAIRS):
        query2, keys2, values2 = query(pair), keys(pair), values(pair)
        place = slice(2 * HD * pair, 2 * HD * (pair + 1))
        scale = jnp.where(
            lanes() < HD, inverse[:, 2 * pair : 2 * pair + 1], inverse[:, 2 * pair + 1 : 2 * pair + 2]
        )
        low = (delta[:, place] * scale).astype(LOW)
        product = low.astype(FULL) * result[:, columns(pair, 2 * HD)].astype(FULL)
        query_turned, low_turned = query2.T, low.T
        delta_query = 0.0
        delta_keys, delta_values = [], []
        for half in range(2):
            weights = shares[2 * pair + half]
            along = jnp.sum(only_half(product, half), axis=1, keepdims=True)
            delta_shares = multiply(only_half(low, half), values2, NT)
            delta_scores = (weights.astype(FULL) * (delta_shares - along)).astype(LOW)
            delta_query = delta_query + multiply(delta_scores, only_half(keys2, half))
            own = slice(HD * half, HD * (half + 1))
            delta_keys.append(multiply(query_turned[own], delta_scores))
            delta_values.append(multiply(low_turned[own], weights))
        keys_turned = (jnp.concatenate(delta_keys, axis=0) * HD**-0.5).astype(LOW)
        values_turned = jnp.concatenate(delta_values, axis=0).astype(LOW)
        put(pair, (delta_query * HD**-0.5).astype(LOW), keys_turned.T, values_turned.T)


def self_parts(triple):
    return tuple(
        (lambda pair, start=part * PAIRS: triple[:, columns(start + pair, 2 * HD)]) for part in range(3)
    )


def put_triple(target):
    def put(pair, *parts):
        for part, value in enumerate(parts):
            target[:, columns(part * PAIRS + pair, 2 * HD)] = value

    return put


def feed(normed, stream, square, tall, active, slope):
    total = stream
    for slab in range(SLABS):
        hidden = multiply(normed, square[EXPAND + slab])
        under = 0.5 + 0.5 * lax.erf(hidden * math.sqrt(0.5))
        bell = BELL * jnp.exp2(hidden * hidden * (-0.5 * LOG2E))
        low = (hidden * under).astype(LOW)
        active[:, columns(slab)] = low
        slope[:, columns(slab)] = (under + hidden * bell).astype(LOW)
        total = total + multiply(low, tall[columns(slab), :])
    return total


def feed_back(delta, stream, gain, square, tall, active, slope, square_sum, tall_sum):
    unit, scale = normalize(stream)
    turned = (unit * gain).astype(LOW).T
    low = delta.astype(LOW)
    delta_normed = 0.0
    for slab in range(SLABS):
        delta_active = multiply(low, tall[columns(slab), :], NT)
        delta_hidden = (delta_active * slope[:, columns(slab)].astype(FULL)).astype(LOW)
        tall_sum[columns(slab), :] += multiply(active[:, columns(slab)], low, TN)
        square_sum[EXPAND + slab] += multiply(turned, delta_hidden)
        delta_normed = delta_normed + multiply(delta_hidden, square[EXPAND + slab], NT)
    delta_stream, delta_gain = norm_back(unit, scale, gain, delta_normed)
    return delta + delta_stream, delta_gain


def self_back(delta, stream, gain, square, triple, shares, inverse, result, delta_triple, square_sum):
    unit, scale = normalize(stream)
    low = delta.astype(LOW)
    square_sum[OUT] += multiply(result[...], low, TN)
    delta_result = multiply(low, square[OUT], NT)
    attend_back(*self_parts(triple), shares, inverse, result, delta_result, put_triple(delta_triple))
    turned = (unit * gain).astype(LOW).T
    delta_normed = 0.0
    for part in range(3):
        chunk = delta_triple[:, columns(part)]
        square_sum[QKV + part] += multiply(turned, chunk)
        delta_normed = delta_normed + multiply(chunk, square[QKV + part], NT)
    delta_stream, delta_gain = norm_back(unit, scale, gain, delta_normed)
    return delta + delta_stream, delta_gain


def project(normed, square, first, count, target):
    for part in range(count):
        target[:, columns(part)] = multiply(normed, square[first + part]).astype(LOW)


def send_sums(square_sum, tall_sum, staging, square_out, tall_out, ready):
    copies = []
    for block in range(BLOCKS + SLABS):
        if block < BLOCKS:
            value, target = square_sum[block], square_out.at[block]
        else:
            rows = columns(block - BLOCKS)
            value, target = tall_sum[rows, :], tall_out.at[rows, :]
        staging(block)[...] = value.astype(LOW)
        copy = pltpu.make_async_copy(staging(block), target, ready.at[block])
        copy.start()
        copies.append(copy)
    for copy in copies:
        copy.wait()


def encode_kernel(
    source_counts, rows, square, tall, gains,
    memory, memory_pair, triple, shares, inverse, result, first, active, slope, second,
    bias,
):
    row = pl.program_id(0)
    square, tall, gains = square.at[0], tall.at[0], gains.at[0]
    stream = rows[0].astype(FULL)
    fill_bias(bias, source_counts, source_counts, row, False)
    normed = (normalize(stream)[0] * gains[0:1, :]).astype(LOW)
    project(normed, square, QKV, 3, triple.at[0])
    attend(*self_parts(triple.at[0]), bias, shares.at[0], inverse.at[0], result.at[0])
    stream = stream + multiply(result[0], square[OUT])
    first[0] = stream
    normed = (normalize(stream)[0] * gains[1:2, :]).astype(LOW)
    stream = feed(normed, stream, square, tall, active.at[0], slope.at[0])
    second[0] = stream
    value = normalize(stream)[0] * gains[2:3, :]
    memory[0] = value
    project(value.astype(LOW), square, CROSS, 2, memory_pair.at[0])


def decode_kernel(
    source_counts, target_counts, rows, memory_pair, cotangent, square, tall, gains,
    output, gradient, delta_pair, square_out, tall_out, gain_out,
    bias, triple, question, self_shares, cross_shares, self_inverse, cross_inverse,
    self_result, cross_result, first, second, active, slope, delta_triple,
    square_sum, tall_sum, gain_sum, ready,
):
    row = pl.program_id(0)
    square, tall, gains = square.at[0], tall.at[0], gains.at[0]
    memory_pair, delta_pair = memory_pair.at[0], delta_pair.at[0]

    @pl.when(row == 0)
    def _():
        square_sum[...] = jnp.zeros(square_sum.shape, FULL)
        tall_sum[...] = jnp.zeros(tall_sum.shape, FULL)
        gain_sum[...] = jnp.zeros(gain_sum.shape, FULL)

    stream = rows[0].astype(FULL)
    fill_bias(bias, target_counts, target_counts, row, True)
    normed = (normalize(stream)[0] * gains[0:1, :]).astype(LOW)
    project(normed, square, QKV, 3, triple)
    attend(*self_parts(triple), bias, self_shares, self_inverse, self_result)
    stream = stream + multiply(self_result[...], square[OUT])
    first[...] = stream

    fill_bias(bias, target_counts, source_counts, row, False)
    normed = (normalize(stream)[0] * gains[1:2, :]).astype(LOW)
    question[...] = multiply(normed, square[CROSS]).astype(LOW)
    cross = (
        lambda pair: question[:, columns(pair, 2 * HD)],
        lambda pair: memory_pair[:, columns(pair, 2 * HD)],
        lambda pair: memory_pair[:, columns(PAIRS + pair, 2 * HD)],
    )
    attend(*cross, bias, cross_shares, cross_inverse, cross_result)
    stream = stream + multiply(cross_result[...], square[CROSS + 1])
    second[...] = stream

    normed = (normalize(stream)[0] * gains[2:3, :]).astype(LOW)
    output[0] = feed(normed, stream, square, tall, active, slope)

    delta, delta_gain = feed_back(
        cotangent[0].astype(FULL), second[...], gains[2:3, :], square, tall, active, slope, square_sum, tall_sum
    )
    gain_sum[2:3, :] += delta_gain

    unit, scale = normalize(first[...])
    low = delta.astype(LOW)
    square_sum[CROSS + 1] += multiply(cross_result[...], low, TN)
    delta_result = multiply(low, square[CROSS + 1], NT)

    def put(pair, query, keys, values):
        delta_triple[:, columns(pair, 2 * HD)] = query
        delta_pair[:, columns(pair, 2 * HD)] = keys
        delta_pair[:, columns(PAIRS + pair, 2 * HD)] = values

    attend_back(*cross, cross_shares, cross_inverse, cross_result, delta_result, put)
    delta_question = delta_triple[:, columns(0)]
    square_sum[CROSS] += multiply((unit * gains[1:2, :]).astype(LOW), delta_question, TN)
    delta_normed = multiply(delta_question, square[CROSS], NT)
    delta_stream, delta_gain = norm_back(unit, scale, gains[1:2, :], delta_normed)
    gain_sum[1:2, :] += delta_gain
    delta = delta + delta_stream

    delta, delta_gain = self_back(
        delta, rows[0].astype(FULL), gains[0:1, :], square, triple, self_shares, self_inverse, self_result,
        delta_triple, square_sum,
    )
    gain_sum[0:1, :] += delta_gain
    gradient[0] = delta

    @pl.when(row == pl.num_programs(0) - 1)
    def _():
        gain_out[...] = gain_sum[...]

        def staging(block):
            return self_shares.at[block] if block < HEADS else cross_shares.at[block - HEADS]

        send_sums(square_sum, tall_sum, staging, square_out, tall_out, ready)


def encode_back_kernel(
    rows, shares_in, triple, inverse, result, first, active, slope, second, delta_pair, square, tall, gains,
    gradient, square_out, tall_out, gain_out,
    shares, spare, delta_triple, square_sum, tall_sum, gain_sum, arrived, ready,
):
    row = pl.program_id(0)
    square, tall, gains = square.at[0], tall.at[0], gains.at[0]
    delta_pair = delta_pair.at[0]
    fetch = pltpu.make_async_copy(shares_in.at[row], shares, arrived)
    fetch.start()

    @pl.when(row == 0)
    def _():
        square_sum[...] = jnp.zeros(square_sum.shape, FULL)
        tall_sum[...] = jnp.zeros(tall_sum.shape, FULL)
        gain_sum[...] = jnp.zeros(gain_sum.shape, FULL)

    unit, scale = normalize(second[0])
    turned = (unit * gains[2:3, :]).astype(LOW).T
    delta_memory = 0.0
    for part in range(2):
        chunk = delta_pair[:, columns(part)]
        square_sum[CROSS + part] += multiply(turned, chunk)
        delta_memory = delta_memory + multiply(chunk, square[CROSS + part], NT)
    delta, delta_gain = norm_back(unit, scale, gains[2:3, :], delta_memory)
    gain_sum[2:3, :] += delta_gain

    delta, delta_gain = feed_back(
        delta, first[0], gains[1:2, :], square, tall, active.at[0], slope.at[0], square_sum, tall_sum
    )
    gain_sum[1:2, :] += delta_gain
    fetch.wait()
    delta, delta_gain = self_back(
        delta, rows[0].astype(FULL), gains[0:1, :], square, triple.at[0], shares, inverse.at[0], result.at[0],
        delta_triple, square_sum,
    )
    gain_sum[0:1, :] += delta_gain
    gradient[0] = delta

    @pl.when(row == pl.num_programs(0) - 1)
    def _():
        gain_out[...] = gain_sum[...]

        def staging(block):
            return shares.at[block] if block < HEADS else spare.at[block - HEADS]

        send_sums(square_sum, tall_sum, staging, square_out, tall_out, ready)


def per_row(*shape):
    return pl.BlockSpec((1,) + shape, lambda row: (row,) + (0,) * len(shape))


def of_layer(layer, *shape):
    return pl.BlockSpec(
        (1,) + shape, lambda row: (layer,) + (0,) * len(shape), pipeline_mode=pl.Buffered(1)
    )


def weight_specs(layer):
    return [of_layer(layer, BLOCKS, D, D), of_layer(layer, FF, D), of_layer(layer, 3, D)]


ANYWHERE = pl.BlockSpec(memory_space=pl.ANY)
SCALARS = pl.BlockSpec(memory_space=pltpu.SMEM)
PARAMS = pltpu.CompilerParams(vmem_limit_bytes=VMEM_LIMIT)


def shape_of(shape, kind):
    return jax.ShapeDtypeStruct(shape, kind)


def sums_scratch():
    return [pltpu.VMEM((BLOCKS, D, D), FULL), pltpu.VMEM((FF, D), FULL), pltpu.VMEM((8, D), FULL)]


def sums_shapes():
    return [shape_of((BLOCKS, D, D), LOW), shape_of((FF, D), LOW), shape_of((8, D), FULL)]


def sums_specs():
    return [ANYWHERE, ANYWHERE, pl.BlockSpec((8, D), lambda row: (0, 0))]


def encode(source_counts, rows, weights):
    count = rows.shape[0]
    kept = [
        ((ROW, D), FULL),
        ((ROW, 2 * D), LOW),
        ((ROW, 3 * D), LOW),
        ((HEADS, ROW, ROW), LOW),
        ((ROW, 2 * HD), FULL),
        ((ROW, D), LOW),
        ((ROW, D), FULL),
        ((ROW, FF), LOW),
        ((ROW, FF), LOW),
        ((ROW, D), FULL),
    ]
    return pl.pallas_call(
        encode_kernel,
        grid=(count,),
        in_specs=[SCALARS, per_row(ROW, D)] + weight_specs(0),
        out_specs=[per_row(*shape) for shape, _ in kept],
        out_shape=[shape_of((count,) + shape, kind) for shape, kind in kept],
        scratch_shapes=[pltpu.VMEM((ROW, ROW), FULL)],
        compiler_params=PARAMS,
        name="encode",
    )(source_counts, rows, *weights)


def decode(source_counts, target_counts, rows, memory_pair, cotangent, weights):
    count = rows.shape[0]
    shares = pltpu.VMEM((HEADS, ROW, ROW), LOW)
    inverse = pltpu.VMEM((ROW, 2 * HD), FULL)
    low = pltpu.VMEM((ROW, D), LOW)
    full = pltpu.VMEM((ROW, D), FULL)
    wide = pltpu.VMEM((ROW, FF), LOW)
    triple = pltpu.VMEM((ROW, 3 * D), LOW)
    return pl.pallas_call(
        decode_kernel,
        grid=(count,),
        in_specs=[SCALARS, SCALARS, per_row(ROW, D), per_row(ROW, 2 * D), per_row(ROW, D)] + weight_specs(1),
        out_specs=[per_row(ROW, D), per_row(ROW, D), per_row(ROW, 2 * D)] + sums_specs(),
        out_shape=[
            shape_of((count, ROW, D), FULL),
            shape_of((count, ROW, D), FULL),
            shape_of((count, ROW, 2 * D), LOW),
        ]
        + sums_shapes(),
        scratch_shapes=[
            pltpu.VMEM((ROW, ROW), FULL), triple, low, shares, shares, inverse, inverse,
            low, low, full, full, wide, wide, triple,
        ]
        + sums_scratch()
        + [pltpu.SemaphoreType.DMA((BLOCKS + SLABS,))],
        compiler_params=PARAMS,
        name="decode",
    )(source_counts, target_counts, rows, memory_pair, cotangent, *weights)


def encode_back(rows, kept, delta_pair, weights):
    count = rows.shape[0]
    triple, shares, inverse, result, first, active, slope, second = kept
    return pl.pallas_call(
        encode_back_kernel,
        grid=(count,),
        in_specs=[
            per_row(ROW, D), ANYWHERE, per_row(ROW, 3 * D), per_row(ROW, 2 * HD), per_row(ROW, D),
            per_row(ROW, D), per_row(ROW, FF), per_row(ROW, FF), per_row(ROW, D), per_row(ROW, 2 * D),
        ]
        + weight_specs(0),
        out_specs=[per_row(ROW, D)] + sums_specs(),
        out_shape=[shape_of((count, ROW, D), FULL)] + sums_shapes(),
        scratch_shapes=[
            pltpu.VMEM((HEADS, ROW, ROW), LOW),
            pltpu.VMEM((BLOCKS + SLABS - HEADS, D, D), LOW),
            pltpu.VMEM((ROW, 3 * D), LOW),
        ]
        + sums_scratch()
        + [pltpu.SemaphoreType.DMA, pltpu.SemaphoreType.DMA((BLOCKS + SLABS,))],
        compiler_params=PARAMS,
        name="encode_back",
    )(rows, shares, triple, inverse, result, first, active, slope, second, delta_pair, *weights)


def gather_weights(square, tall, gains, shards):
    axes = ("pipe", "dp")
    every_square = lax.all_gather(square, axes, axis=0, tiled=False)
    every_tall = lax.all_gather(tall, axes, axis=0, tiled=False)
    every_gain = lax.all_gather(gains.astype(LOW), axes, axis=0, tiled=False)
    every_square = every_square.reshape(2, shards, BLOCKS, D // shards, D)
    every_gain = every_gain.reshape(2, shards, 3, D // shards)
    return (
        jnp.swapaxes(every_square, 1, 2).reshape(2, BLOCKS, D, D),
        every_tall.reshape(2, FF, D),
        jnp.swapaxes(every_gain, 1, 2).reshape(2, 3, D).astype(FULL),
    )


def scatter_sums(square, tall, gains, shards):
    axes = ("pipe", "dp")
    square = jnp.swapaxes(square.reshape(2, BLOCKS, shards, D // shards, D), 1, 2)
    gains = jnp.swapaxes(gains.reshape(2, 3, shards, D // shards), 1, 2)
    square = square.reshape(2 * shards, BLOCKS, D // shards, D)
    tall = tall.reshape(2 * shards, FF // shards, D)
    gains = gains.reshape(2 * shards, 3, D // shards)
    return tuple(
        lax.psum_scatter(value, axes, scatter_dimension=0, tiled=False).astype(FULL)
        for value in (square, tall, gains)
    )


def swap(value):
    return lax.ppermute(value, "pipe", [(0, 1), (1, 0)])


def blocks_of(value):
    return [value[:, start : start + D] for start in range(0, value.shape[1], D)]


def local(
    section_input,
    attention_in,
    attention_out,
    cross_weights,
    expand,
    contract,
    norm_gains,
    source_lengths,
    target_lengths,
    cotangent,
):
    section = lax.axis_index("pipe")
    shards = lax.axis_size("dp")
    rows = section_input[0]
    count = rows.shape[0] // 2
    start = section * count

    def part(value, first):
        return lax.dynamic_slice_in_dim(value, first, count, axis=0)

    mine = part(rows, start)
    other = swap(part(rows, count - start))
    source_rows = jnp.where(section == 0, mine, other)
    target_rows = jnp.where(section == 0, other, mine)
    source_counts = part(source_lengths, start)
    target_counts = part(target_lengths, start)

    square = jnp.stack(
        blocks_of(attention_in[0]) + [attention_out[0]] + blocks_of(cross_weights[0]) + blocks_of(expand[0])
    ).astype(LOW)
    weights = gather_weights(square, contract[0].astype(LOW), norm_gains[0], shards)

    memory, memory_pair, *kept = encode(source_counts, source_rows, weights)
    output, target_gradient, delta_pair, *decoder_sums = decode(
        source_counts, target_counts, target_rows, memory_pair, part(cotangent, start), weights
    )
    source_gradient, *encoder_sums = encode_back(source_rows, kept, delta_pair, weights)

    def settle(source, target):
        own = jnp.where(section == 0, source, target)
        away = swap(jnp.where(section == 0, target, source).astype(LOW)).astype(FULL)
        whole = jnp.zeros((2 * count, ROW, D), FULL)
        whole = lax.dynamic_update_slice_in_dim(whole, own, start, axis=0)
        return lax.dynamic_update_slice_in_dim(whole, away, count - start, axis=0)[None]

    section_output = settle(memory, output)
    input_gradient = settle(source_gradient, target_gradient)

    square, tall, gains = (jnp.stack(pair) for pair in zip(encoder_sums, decoder_sums))
    square, tall, gains = scatter_sums(square, tall, gains[:, :3], shards)

    def joined(first, last):
        return jnp.concatenate([square[block] for block in range(first, last)], axis=1)[None]

    return (
        section_output,
        input_gradient,
        joined(QKV, OUT),
        joined(OUT, CROSS),
        joined(CROSS, EXPAND),
        joined(EXPAND, BLOCKS),
        tall[None],
        gains[None],
    )


def solution(mesh):
    in_specs = (
        P("pipe", "dp", None, None),
        P("pipe", "dp", None),
        P("pipe", "dp", None),
        P("pipe", "dp", None),
        P("pipe", "dp", None),
        P("pipe", "dp", None),
        P("pipe", None, "dp"),
        P("dp", None),
        P("dp", None),
        P("dp", None, None),
    )
    out_specs = (
        P("pipe", "dp", None, None),
        P("pipe", "dp", None, None),
        P("pipe", "dp", None),
        P("pipe", "dp", None),
        P("pipe", "dp", None),
        P("pipe", "dp", None),
        P("pipe", "dp", None),
        P("pipe", None, "dp"),
    )
    return jax.shard_map(local, mesh=mesh, in_specs=in_specs, out_specs=out_specs, check_vma=False)
```

time: 1420 us -> 645 us (0.45)
  matrix products: 350 us -> 0 us
  waiting for transfers between devices: 633 us -> 306 us
  starting transfers between devices: 171 us -> 5.56 us
  Pallas kernels: 0 us -> 162 us
  local copies, waits for them, and re-layouts: 105 us -> 34.3 us
  loops' own time: 38.5 us -> 0 us
  blocking collectives: 43.4 us -> 80.9 us
  other arithmetic: 52.9 us -> 34.4 us
    dot_general x100 -> x0, matrix products: 319 us -> none  [the longest x32 144 us: matmul(): return jnp.dot(left, right, preferred_element_type=jnp.float32)]
    reduce_scatter x5 -> x2, waiting for transfers between devices: 347 us -> 179 us  [scatter_sums(): lax.psum_scatter(value, axes, scatter_dimension=0, tiled=False).astype(FULL)]
    ppermute x5 -> x3, starting transfers between devices: 170 us -> 5.4 us  [swap(): return lax.ppermute(value, 'pipe', [(0, 1), (1, 0)])]
    pallas_call x0 -> x3, Pallas kernels: none -> 162 us  [the longest x1 97.8 us: decode(): pl.pallas_call(decode_kernel, grid=(count,), in_specs=[SCALARS, SCALARS,...]
    ppermute x5 -> x3, waiting for transfers between devices: 114 us -> 33.8 us  [swap(): return lax.ppermute(value, 'pipe', [(0, 1), (1, 0)])]
    unnamed x11 -> x4, waiting for transfers between devices: 53.4 us -> 0.07 us
    slice x38 -> x1, local copies, waits for them, and re-layouts: 49 us -> 0.01 us  [local(): square, tall, gains = scatter_sums(square, tall, gains[:, :3], shards)]
    unnamed x0 -> x1, blocking collectives: none -> 40 us
  transfers between devices with their start and end apart: 15 -> 7, of which waited for: 14 -> 6; matrix products, arithmetic and copies ran while one was open for 1% -> 9% of each run, Pallas kernels for 0% -> 0%
where the time goes in v1:
time: 645 us; the launch traced here: 637 us
  waiting for transfers between devices  306 us (47%)
  Pallas kernels  162 us (25%)
  blocking collectives  80.9 us (13%)
  other arithmetic  34.4 us (5%)
  local copies, waits for them, and re-layouts  34.3 us (5%)
  between operations  14.2 us (2%)
    reduce_scatter x2, waiting for transfers between devices, scatter_sums(): lax.psum_scatter(value, axes, scatter_dimension=0, tiled=False).astype(FULL)  179 us
    pallas_call x1, Pallas kernels, decode(): pl.pallas_call(decode_kernel, grid=(count,), in_specs=[SCALARS, SCALARS,...  97.8 us
    all_gather x1, waiting for transfers between devices, gather_weights(): every_tall = lax.all_gather(tall, axes, axis=0, tiled=False)  53.9 us
    all_gather x1, blocking collectives, gather_weights(): every_gain = lax.all_gather(gains.astype(LOW), axes, axis=0, tiled=False)  40.9 us
    pallas_call x1, Pallas kernels, encode_back(): pl.pallas_call(encode_back_kernel, grid=(count,), in_specs=[per_row(ROW,...  40.4 us
    unnamed x1, blocking collectives  40 us
    all_gather x1, waiting for transfers between devices, gather_weights(): every_square = lax.all_gather(square, axes, axis=0, tiled=False)  38.9 us
    ppermute x3, waiting for transfers between devices, swap(): return lax.ppermute(value, 'pipe', [(0, 1), (1, 0)])  33.8 us
  transfers between devices with their start and end apart: 7, of which 6 were waited for; matrix products, arithmetic and copies ran while one was open for 9% of the time, Pallas kernels for 0%

profile of v1, /device:TPU:0, one launch (start us, length us, event | category | flops | bytes accessed | tf_op | source)
XLA Modules:
  0.0 636.8 jit_solution(4478810051833163796)
XLA Ops:
  7.2 0.0 copy-start.4
  7.2 0.0 copy-start.8
  7.2 0.0 copy-start.10
  7.2 0.0 copy-start.9
  7.2 0.0 all-gather.3.cloned.1.call-start
  7.3 1.1 convert_bitcast_fusion.1
  8.4 0.9 convert_bitcast_fusion.2
  9.3 0.8 bitcast_dynamic-update-slice_fusion.2
  10.1 1.0 convert_bitcast_fusion
  11.2 0.0 copy-start.5
  11.2 0.7 copy-done.5
  11.9 0.0 all-gather.3.cloned.1.call-update
  11.9 0.0 all-gather.5.cloned.1.call-start
  12.0 1.6 convert_element_type.41
  13.6 0.0 all-gather.5.cloned.1.call-update
  13.6 0.0 reduce-scatter.5.cloned.1.call-start
  13.7 2.3 dynamic-slice_bitcast_fusion
  15.9 2.9 collective-permute-start
  18.9 0.0 copy-done.8
  18.9 40.9 %all_gather.14 = bf16[32,3,32]{2,1,0:T(4,128)(2,1)S(1)} all-gather(bf16[1,3,32]{2,1,0:T(4,128)(2,1)S(1)} %copy.40), channel_id=1, replica_groups=mesh['pipe'=2,'dp'=16] {'pipe','dp'}, dimensions={0}, use_global_device_ids=true | all-gather | bytes 6336 | tf_op jit(solution)/shard_map/all_gather | solution.py:479
  59.8 0.1 reshape.242
  59.9 0.6 copy.31.gains
  60.5 0.0 copy-done.10
  60.5 0.6 constant_dynamic-slice_fusion.1
  61.1 2.3 constant_dynamic-slice_fusion.cotangent
  63.4 0.0 collective-permute-done
  63.4 1.5 bitcast_select_fusion
  64.8 38.9 %all-gather.3.cloned.1.call-done = bf16[32,10,32,512]{3,2,1,0:T(8,128)(2,1)} async-done(((bf16[1,10,32,512]{3,2,1,0:T(8,128)(2,1)}), bf16[32,10,32,512]{3,2,1,0:T(8,128)(2,1)}) %all-gather.3.cloned.1.call-update) | async-done | bytes 10485776 | tf_op jit(solution)/shard_map/all_gather | solution.py:477
  103.8 10.2 %copy.28 = bf16[2,16,10,32,512]{4,3,1,2,0:T(8,128)(2,1)} copy(bf16[2,16,10,32,512]{4,3,2,1,0:T(8,128)(2,1)} %bitcast.122) | data formatting | bytes 20971520 | tf_op jit(solution)/shard_map/reshape | solution.py:480
  113.9 53.9 %all-gather.5.cloned.1.call-done = bf16[32,128,512]{2,1,0:T(8,128)(2,1)} async-done(((bf16[1,128,512]{2,1,0:T(8,128)(2,1)}), bf16[32,128,512]{2,1,0:T(8,128)(2,1)}) %all-gather.5.cloned.1.call-update) | async-done | bytes 4194320 | tf_op jit(solution)/shard_map/all_gather | solution.py:478
  167.8 23.7 %encode.1 = (f32[2,512,512]{2,1,0:T(8,128)}, bf16[2,512,1024]{2,1,0:T(8,128)(2,1)}, bf16[2,512,1536]{2,1,0:T(8,128)(2,1)}, bf16[2,8,512,512]{3,2,1,0:T(8,128)(2,...) custom-call(s32[2,4]{1,0:T(2,128)} %get-tuple-element.69.source_coun, ...), custom_call_target="tpu_custom_call" | custom-call | tf_op jit(solution)/shard_map/encode/pallas_call | solution.py:408
  191.5 97.8 %decode.1 = (f32[2,512,512]{2,1,0:T(8,128)}, f32[2,512,512]{2,1,0:T(8,128)}, bf16[2,512,1024]{2,1,0:T(8,128)(2,1)}, bf16[10,512,512]{2,1,0:T(8,128)(2,1)}, bf16[2048,512]{1,0:T(8,128)(2,1)}, /*index=5*/f32[8,512]{1,0:T(8,128)}) custom-call(s32[2,4]{1,0:T(2,128)} %get-tuple-element.69.source_counts, s32[2,4]{1,0:T(2,128)} %get-tuple-element.68.target_counts, ...), custom_call_target="tpu_custom_call" | custom-call | tf_op jit(solution)/shard_map/decode/pallas_call | solution.py:428
  289.3 40.4 %encode_back.1 = (f32[2,512,512]{2,1,0:T(8,128)}, bf16[10,512,512]{2,1,0:T(8,128)(2,1)}, bf16[2048,512]{1,0:T(8,128)(2,1)}, f32[8,512]{1,0:T(8,128)}) custom-call(bf16[2,512,512]{2,1,0:T(8,128)(2,1)} %get-tuple-element.57.rows, bf16[2,8,512,512]{3,2,1,0:T(8,128)(2,1)} %get-tuple-element.31.shares_in, bf16[2,512,1536]{2,1,0:T(8,128)(2,1)} %get-tuple-element.32.triple, ...), custom_call_target="tpu_custom_call" | custom-call | tf_op jit(solution)/shard_map/encode_back/pallas_call | solution.py:453
  329.7 4.5 pad_maximum_fusion
  334.3 0.0 reduce-scatter.5.cloned.1.call-update
  334.3 0.0 reduce-scatter.3.cloned.1.call-start
  334.3 8.9 %maximum_bitcast_fusion = bf16[2,16,10,32,512]{4,3,1,2,0:T(8,128)(2,1)} fusion(bf16[1,10,16,32,512]{4,3,2,1,0:T(8,128)(2,1)} %bitcast.123, bf16[1,10,16,32,512]{4,3,2,1,0:T(8,128)(2,1)} %bitcast.124), kind=kLoop, calls=%fused_computation | loop fusion | flops 5242880 | bytes 20971520 | tf_op jit(solution)/shard_map/transpose | solution.py:491
  343.2 10.2 %copy.34 = bf16[2,16,10,32,512]{4,3,2,1,0:T(8,128)(2,1)} copy(bf16[2,16,10,32,512]{4,3,1,2,0:T(8,128)(2,1)} %maximum_bitcast_fusion) | data formatting | bytes 20971520 | tf_op jit(solution)/shard_map/transpose | solution.py:491
  353.4 0.0 reduce-scatter.3.cloned.1.call-update
  353.5 0.7 copy-done.6
  354.1 0.0 copy-done.7
  354.2 0.1 reshape.237
  354.3 40.0 %all-reduce = f32[32,3,32]{2,1,0:T(4,128)S(1)} all-reduce(f32[32,3,32]{2,1,0:T(4,128)S(1)} %copy.36), channel_id=4, replica_groups=mesh['pipe'=2,'dp'=16] {'pipe','dp'}, use_global_device_ids=true, to_apply=%region_2.3.clone | all-reduce | flops 3072 | bytes 24576
  394.4 0.6 copy.37
  394.9 2.0 select_convert_fusion
  396.9 2.4 collective-permute-start.2
  399.3 0.6 select_convert_fusion.1
  399.9 0.1 collective-permute-start.1
  400.0 2.5 broadcast_in_dim.26.clone.1
  402.5 1.8 bitcast_dynamic-update-slice_fusion
  404.3 2.5 broadcast_in_dim.26.clone
  406.9 1.8 bitcast_dynamic-update-slice_fusion.1
  408.7 14.7 %collective-permute-done.2 = bf16[2,512,512]{2,1,0:T(8,128)(2,1)S(1)} collective-permute-done((bf16[2,512,512]{2,1,0:T(8,128)(2,1)S(1)}, bf16[2,512,512]{2,1,0:T(8,128)(2,1)S(1)}, u32[]{:S(2)}, u32[]{:S(2)}) %collective-permute-start.2) | collective-permute-done | bytes 1048608 | tf_op jit(solution)/shard_map/ppermute | solution.py:503
  423.4 1.6 convert_dynamic-update-slice_fusion
  425.0 19.1 %collective-permute-done.1 = bf16[2,512,512]{2,1,0:T(8,128)(2,1)S(1)} collective-permute-done((bf16[2,512,512]{2,1,0:T(8,128)(2,1)S(1)}, bf16[2,512,512]{2,1,0:T(8,128)(2,1)S(1)}, u32[]{:S(2)}, u32[]{:S(2)}) %collective-permute-start.1) | collective-permute-done | bytes 1048608 | tf_op jit(solution)/shard_map/ppermute | solution.py:503
  444.0 1.6 convert_dynamic-update-slice_fusion.1
  445.7 29.8 %reduce-scatter.5.cloned.1.call-done = bf16[1,128,512]{2,1,0:T(8,128)(2,1)} async-done(((bf16[32,128,512]{2,1,0:T(8,128)(2,1)}), bf16[1,128,512]{2,1,0:T(8,128)(2,1)}) %reduce-scatter.5.cloned.1.call-update) | async-done | bytes 131088 | tf_op jit(solution)/shard_map/reduce_scatter | solution.py:497
  475.5 1.6 convert_element_type.50
  477.1 149.1 %reduce-scatter.3.cloned.1.call-done = bf16[1,10,32,512]{3,2,1,0:T(8,128)(2,1)} async-done(((bf16[32,10,32,512]{3,2,1,0:T(8,128)(2,1)}), bf16[1,10,32,512]{3,2,1,0:T(8,128)(2,1)}) %reduce-scatter.3.cloned.1.call-update) | async-done | bytes 327696 | tf_op jit(solution)/shard_map/reduce_scatter | solution.py:497
  626.2 1.0 convert_element_type.49
  627.3 0.7 slice_bitcast_fusion.3
  628.0 0.7 maximum_bitcast_fusion.3
  628.6 0.7 maximum_bitcast_fusion.2
  629.3 0.7 maximum_bitcast_fusion.1
  (27 shorter events, 0.1 us)
Async XLA Ops:
  7.2 56.2 %copy-start.4 = (bf16[1,4,512,512]{3,2,1,0:T(8,128)(2,1)S(1)}, bf16[1,4,512,512]{3,2,1,0:T(8,128)(2,1)}, u32[]{:S(2)}) copy-start(bf16[1,4,512,512]{3,2,1,0:T(8,128)(2,1)} %param.10) | copy-start | bytes 6291460
  7.2 11.7 %copy-start.8 = (f32[1,3,32]{2,0,1:T(1,128)S(1)}, f32[1,3,32]{2,0,1:T(1,128)}, u32[]{:S(2)}) copy-start(f32[1,3,32]{2,0,1:T(1,128)} %param.16) | copy-start | bytes 1156
  7.2 53.3 %copy-start.10 = (s32[4,4]{1,0:T(4,128)S(1)}, s32[4,4]{1,0:T(4,128)}, u32[]{:S(2)}) copy-start(s32[4,4]{1,0:T(4,128)} %param.17) | copy-start | bytes 196
  7.2 53.3 %copy-start.9 = (s32[4,4]{1,0:T(4,128)S(1)}, s32[4,4]{1,0:T(4,128)}, u32[]{:S(2)}) copy-start(s32[4,4]{1,0:T(4,128)} %param.18) | copy-start | bytes 196
  7.2 96.5 %all-gather.3.cloned.1.call-start = ((), (), s32[]{:S(2)}) async-start(), calls=%async_computation.2 | async-start | bytes 10813440 | tf_op jit(solution)/shard_map/all_gather | solution.py:477
  11.2 0.7 copy-start.5
  11.9 155.9 %all-gather.5.cloned.1.call-start = ((), (), s32[]{:S(2)}) async-start(), calls=%async_computation.3 | async-start | bytes 4325376 | tf_op jit(solution)/shard_map/all_gather | solution.py:478
  13.6 461.8 %reduce-scatter.5.cloned.1.call-start = ((), (), s32[]{:S(2)}) async-start(), calls=%async_computation.5 | async-start | bytes 4325376 | tf_op jit(solution)/shard_map/reduce_scatter | solution.py:497
  15.9 47.4 %collective-permute-start = (bf16[2,512,512]{2,1,0:T(8,128)(2,1)}, bf16[2,512,512]{2,1,0:T(8,128)(2,1)S(1)}, u32[]{:S(2)}, u32[]{:S(2)}) collective-permute-start(bf16[2,512,512]{2,1,0:T(8,128)(2,1)} %dynamic-slice_bitcast_fusion), channel_id=1, source_target_pairs={{0,16},{16,0},{1,17},{17,1},{2,18},{18,2},{3,19},{19,3},{4,20},{20... | collective-permute-start | bytes 3145736 | tf_op jit(solution)/shard_map/ppermute | solution.py:503
  334.3 291.9 %reduce-scatter.3.cloned.1.call-start = ((), (), s32[]{:S(2)}) async-start(), calls=%async_computation.4 | async-start | bytes 10813440 | tf_op jit(solution)/shard_map/reduce_scatter | solution.py:497
  353.4 0.7 copy-start.6
  353.4 0.7 copy-start.7
  353.4 45.8 %copy-start = (f32[2,512,512]{2,1,0:T(8,128)S(1)}, f32[2,512,512]{2,1,0:T(8,128)}, u32[]{:S(2)}) copy-start(f32[2,512,512]{2,1,0:T(8,128)} %get-tuple-element.28) | copy-start | bytes 6291460
  394.3 4.9 copy-start.1
  396.9 26.4 %collective-permute-start.2 = (bf16[2,512,512]{2,1,0:T(8,128)(2,1)S(1)}, bf16[2,512,512]{2,1,0:T(8,128)(2,1)S(1)}, u32[]{:S(2)}, u32[]{:S(2)}) collective-permute-start(bf16[2,512,512]{2,1,0:T(8,128)(2,1)S(1)} %select_convert_fusion), channel_id=1, source_target_pairs={{0,16},{16,0},{1,17},{17,1},{2,18},{18,2},{3,19},{19,3},{4,20},{20... | collective-permute-start | bytes 3145736 | tf_op jit(solution)/shard_map/ppermute | solution.py:503
  399.3 3.2 copy-start.2
  399.3 3.2 copy-start.3
  399.9 44.2 %collective-permute-start.1 = (bf16[2,512,512]{2,1,0:T(8,128)(2,1)S(1)}, bf16[2,512,512]{2,1,0:T(8,128)(2,1)S(1)}, u32[]{:S(2)}, u32[]{:S(2)}) collective-permute-start(bf16[2,512,512]{2,1,0:T(8,128)(2,1)S(1)} %select_convert_fusion.1), channel_id=1, source_target_pairs={{0,16},{16,0},{1,17},{17,1},{2,18},{18,2},{3,19},{19,3},{4,20},{20... | collective-permute-start | bytes 3145736 | tf_op jit(solution)/shard_map/ppermute | solution.py:503
Sparse Core Ops, SparseCore 0:
  12.0 91.6 all-gather.2
  107.2 60.5 all-gather.4
  334.4 141.0 reduce-scatter.4
  477.6 148.5 reduce-scatter.2

commit v2 on v1

--- a/solution.py
+++ b/solution.py
@@ -472,10 +472,208 @@
     )(rows, shares, triple, inverse, result, first, active, slope, second, delta_pair, *weights)
 
 
-def gather_weights(square, tall, gains, shards):
+MESH = pl.DeviceIdType.MESH
+UNITS = BLOCKS + SLABS
+UNIT = 32
+DEPTHS, SIDES, CORES = 4, 2, 2
+
+
+class Place:
+    def __init__(self):
+        self.layer = lax.axis_index("pipe")
+        self.rank = lax.axis_index("dp")
+        self.core = self.rank % CORES
+        self.side = self.rank // CORES % SIDES
+        self.depth = self.rank // (CORES * SIDES)
+
+    def sibling(self):
+        return (self.layer, self.rank + 1 - 2 * self.core)
+
+    def across_side(self):
+        return (self.layer, self.rank + CORES * (1 - 2 * self.side))
+
+    def across_layer(self):
+        return (1 - self.layer, self.rank)
+
+    def other_depth(self, step):
+        return (self.depth + step) % DEPTHS
+
+    def along_depth(self, step):
+        return (self.layer, self.rank + CORES * SIDES * (self.other_depth(step) - self.depth))
+
+    def greet(self):
+        partners = [self.sibling(), self.across_side(), self.across_layer()]
+        partners += [self.along_depth(step) for step in range(1, DEPTHS)]
+        barrier = pltpu.get_barrier_semaphore()
+        for partner in partners:
+            pl.semaphore_signal(barrier, inc=1, device_id=partner, device_id_type=MESH)
+        pl.semaphore_wait(barrier, len(partners))
+
+
+def push(source, target, sent, arrived, device):
+    copy = pltpu.make_async_remote_copy(
+        src_ref=source, dst_ref=target, send_sem=sent, recv_sem=arrived, device_id=device, device_id_type=MESH
+    )
+    copy.start()
+    return copy
+
+
+def layer_first(unit):
+    return unit % 4 != 3
+
+
+def gather_kernel(
+    attention_in, attention_out, cross, expand, contract, gains, rows,
+    square, tall, every_gain, away,
+    own, own_done, depth_sent, depth_done, first_sent, first_done, last_sent, last_done,
+    core_sent, core_done, gain_sent, gain_done, gain_own, row_sent, row_done,
+):
+    place = Place()
+    layer, depth, side, core = place.layer, place.depth, place.side, place.core
+    count = away.shape[0]
+    sources = [attention_in.at[:, columns(j)] for j in range(3)] + [attention_out]
+    sources += [cross.at[:, columns(j)] for j in range(2)] + [expand.at[:, columns(j)] for j in range(SLABS)]
+    sources += [contract.at[columns(j, UNIT), :] for j in range(SLABS)]
+
+    def spot(unit, *index):
+        if unit < BLOCKS:
+            return square.at[(index[0], unit) + index[1:]]
+        return tall.at[index + (unit - BLOCKS,)]
+
+    place.greet()
+    swap_rows = push(
+        rows.at[pl.ds(count - layer * count, count)], away, row_sent, row_done, place.across_layer()
+    )
+    everything = slice(None)
+    owned, deep, first, last, shared = [], [], [], [], []
+
+    mine = every_gain.at[layer, depth, side, core]
+    gain_copy = pltpu.make_async_copy(gains, mine, gain_own)
+    gain_copy.start()
+    gain_pushes = [
+        push(gains, mine, gain_sent.at[step - 1], gain_done.at[step - 1], place.along_depth(step))
+        for step in range(1, DEPTHS)
+    ]
+
+    def begin(unit):
+        own[unit] = sources[unit][...].astype(LOW)
+        target = spot(unit, layer, depth, side, core)
+        copy = pltpu.make_async_copy(own.at[unit], target, own_done.at[unit])
+        copy.start()
+        owned.append(copy)
+        deep.append(
+            [
+                push(
+                    own.at[unit], target, depth_sent.at[unit, step - 1], depth_done.at[unit, step - 1],
+                    place.along_depth(step),
+                )
+                for step in range(1, DEPTHS)
+            ]
+        )
+
+    def cross_first(unit):
+        owned[unit].wait()
+        for copy in deep[unit]:
+            copy.wait_recv()
+        block = spot(unit, layer, everything, side, core)
+        target = place.across_layer() if layer_first(unit) else place.across_side()
+        first.append(push(block, block, first_sent.at[unit], first_done.at[unit], target))
+
+    def cross_last(unit):
+        first[unit].wait_recv()
+        if layer_first(unit):
+            block, target = spot(unit, everything, everything, side, core), place.across_side()
+        else:
+            block, target = spot(unit, layer, everything, everything, core), place.across_layer()
+        last.append(push(block, block, last_sent.at[unit], last_done.at[unit], target))
+
+    def share(unit):
+        last[unit].wait_recv()
+        block = spot(unit, everything, everything, everything, core)
+        shared.append(push(block, block, core_sent.at[unit], core_done.at[unit], place.sibling()))
+
+    def gain_step(position):
+        whole = every_gain.at[layer, :, side, core]
+        if position == 0:
+            gain_copy.wait()
+            for copy in gain_pushes:
+                copy.wait_recv()
+            target = place.across_layer()
+        elif position == 1:
+            gain_pushes[-1].wait_recv()
+            whole, target = every_gain.at[:, :, side, core], place.across_side()
+        else:
+            gain_pushes[-1].wait_recv()
+            whole, target = every_gain.at[:, :, :, core], place.sibling()
+        slot = DEPTHS - 1 + position
+        gain_pushes.append(push(whole, whole, gain_sent.at[slot], gain_done.at[slot], target))
+
+    ahead, gap = 4, 2
+    for unit in range(ahead):
+        begin(unit)
+    for step in range(UNITS + 2 * gap):
+        if step + ahead < UNITS:
+            begin(step + ahead)
+        if step < UNITS:
+            cross_first(step)
+        if 0 <= step - gap < UNITS:
+            cross_last(step - gap)
+        if 0 <= step - 2 * gap < UNITS:
+            share(step - 2 * gap)
+        if step < 3:
+            gain_step(step)
+    for unit in range(UNITS):
+        shared[unit].wait()
+        last[unit].wait_send()
+        first[unit].wait_send()
+        for copy in deep[unit]:
+            copy.wait_send()
+    gain_pushes[-1].wait_recv()
+    for copy in gain_pushes:
+        copy.wait_send()
+    swap_rows.wait()
+
+
+def gather_near(weights, gains, rows):
+    count = rows.shape[0] // 2
+    shards = DEPTHS * SIDES * CORES
+    tile = jnp.tile(gains.astype(LOW), (1, 4))
+    lane_part = lax.broadcasted_iota(jnp.int32, tile.shape, 1) // UNIT
+    tile = jnp.where(lane_part == lax.axis_index("dp") % 4, tile, jnp.zeros_like(tile))
+    tile = jnp.pad(tile, ((0, 16 - tile.shape[0]), (0, 0)))
+    dma = pltpu.SemaphoreType.DMA
+    vmem = pl.BlockSpec(memory_space=pltpu.VMEM)
+    square, tall, every_gain, away = pl.pallas_call(
+        gather_kernel,
+        in_specs=[vmem] * 6 + [ANYWHERE],
+        out_specs=[ANYWHERE] * 4,
+        out_shape=[
+            shape_of((2, BLOCKS, DEPTHS, SIDES, CORES, UNIT, D), LOW),
+            shape_of((2, DEPTHS, SIDES, CORES, SLABS, UNIT, D), LOW),
+            shape_of((2, DEPTHS, SIDES, CORES, 16, 128), LOW),
+            shape_of((count, ROW, D), LOW),
+        ],
+        scratch_shapes=[
+            pltpu.VMEM((UNITS, UNIT, D), LOW), dma((UNITS,)),
+            dma((UNITS, 3)), dma((UNITS, 3)), dma((UNITS,)), dma((UNITS,)), dma((UNITS,)), dma((UNITS,)),
+            dma((UNITS,)), dma((UNITS,)), dma((6,)), dma((6,)), dma, dma, dma,
+        ],
+        compiler_params=pltpu.CompilerParams(
+            vmem_limit_bytes=VMEM_LIMIT, collective_id=0, has_side_effects=True
+        ),
+        name="gather",
+    )(*weights, tile, rows)
+    every_gain = every_gain.reshape(2, 4, 4, 16, 128).astype(FULL).sum(axis=2)[:, :, :3]
+    every_gain = jnp.swapaxes(every_gain, 1, 2).reshape(2, 3, D)
+    return (square.reshape(2, BLOCKS, D, D), tall.reshape(2, FF, D), every_gain), away
+
+
+def gather_weights(weights, gains, shards):
+    attention_in, attention_out, cross, expand, contract = weights
+    square = jnp.stack(blocks_of(attention_in) + [attention_out] + blocks_of(cross) + blocks_of(expand)).astype(LOW)
     axes = ("pipe", "dp")
     every_square = lax.all_gather(square, axes, axis=0, tiled=False)
-    every_tall = lax.all_gather(tall, axes, axis=0, tiled=False)
+    every_tall = lax.all_gather(contract.astype(LOW), axes, axis=0, tiled=False)
     every_gain = lax.all_gather(gains.astype(LOW), axes, axis=0, tiled=False)
     every_square = every_square.reshape(2, shards, BLOCKS, D // shards, D)
     every_gain = every_gain.reshape(2, shards, 3, D // shards)
@@ -486,10 +684,206 @@
     )
 
 
-def scatter_sums(square, tall, gains, shards):
+def add_low(left, right):
+    return (left.astype(FULL) + right.astype(FULL)).astype(LOW)
+
+
+def scatter_kernel(
+    source_square, source_tall, source_gain, target_square, target_tall, target_gain,
+    square_out, tall_out, gain_out,
+    total, from_core, from_side, from_layer, middle, from_last, ending, from_depth, gain_total, gain_parts,
+    loaded, core_sent, core_done, first_sent, first_done, last_sent, last_done, depth_sent, depth_done,
+    gain_sent, gain_done,
+):
+    place = Place()
+    layer, depth, side, core = place.layer, place.depth, place.side, place.core
+    everything = slice(None)
+
+    def spot(which, unit, owner):
+        if unit < BLOCKS:
+            return (source_square, target_square)[which].at[unit, :, :, owner]
+        return (source_tall, target_tall)[which].at[:, :, owner, unit - BLOCKS]
+
+    loads, cores, first, last, deep, gains = [], [], [], [], [], []
+
+    def begin(unit):
+        for which in range(2):
+            cores.append(
+                push(
+                    spot(which, unit, 1 - core), from_core.at[unit, which], core_sent.at[unit, which],
+                    core_done.at[unit, which], place.sibling(),
+                )
+            )
+            load = pltpu.make_async_copy(spot(which, unit, core), total.at[unit, which], loaded.at[unit, which])
+            load.start()
+            loads.append(load)
+
+    def cross_first(unit):
+        for which in range(2):
+            loads[2 * unit + which].wait()
+            cores[2 * unit + which].wait_recv()
+
+            def add(step, carry):
+                total[unit, which, step] = add_low(total[unit, which, step], from_core[unit, which, step])
+                return carry
+
+            lax.fori_loop(0, DEPTHS, add, 0)
+        if layer_first(unit):
+            block, landing, target = total.at[unit, :, :, 1 - side], from_side.at[unit], place.across_side()
+        else:
+            block, landing, target = total.at[unit, 1 - layer], from_layer.at[unit], place.across_layer()
+        first.append(push(block, landing, first_sent.at[unit], first_done.at[unit], target))
+
+    def cross_last(unit):
+        first[unit].wait_recv()
+        if layer_first(unit):
+
+            def add(step, carry):
+                which, row = step // DEPTHS, step % DEPTHS
+                middle[unit, which, row] = add_low(total[unit, which, row, side], from_side[unit, which, row])
+                return carry
+
+            target = place.across_layer()
+            source = middle.at[unit, 1 - layer]
+        else:
+
+            def add(step, carry):
+                which, row = step // DEPTHS, step % DEPTHS
+                middle[unit, which, row] = add_low(total[unit, layer, row, which], from_layer[unit, row, which])
+                return carry
+
+            target = place.across_side()
+            source = middle.at[unit, 1 - side]
+        lax.fori_loop(0, 2 * DEPTHS, add, 0)
+        last.append(push(source, from_last.at[unit], last_sent.at[unit], last_done.at[unit], target))
+
+    def along_depth(unit):
+        last[unit].wait_recv()
+        kept = layer if layer_first(unit) else side
+        ending[unit] = add_low(middle[unit, kept], from_last[unit])
+        deep.append(
+            [
+                push(
+                    ending.at[unit, place.other_depth(step)], from_depth.at[unit, step - 1],
+                    depth_sent.at[unit, step - 1], depth_done.at[unit, step - 1], place.along_depth(step),
+                )
+                for step in range(1, DEPTHS)
+            ]
+        )
+
+    def finish(unit):
+        value = ending[unit, depth].astype(FULL)
+        for step in range(1, DEPTHS):
+            deep[unit][step - 1].wait_recv()
+            value = value + from_depth[unit, step - 1].astype(FULL)
+        if unit < BLOCKS:
+            square_out[unit] = value
+        else:
+            tall_out[columns(unit - BLOCKS, UNIT), :] = value
+
+    def gain_step(position):
+        if position == 0:
+            for which, gain in enumerate((source_gain, target_gain)):
+                for row in range(DEPTHS):
+                    gain_total[0, which, row] = gain[:, columns(row, 128)]
+            source, target = gain_total.at[0], place.sibling()
+        elif position == 1:
+            gains[0].wait_recv()
+            gain_total[1] = gain_total[0] + gain_parts[0]
+            source, target = gain_total.at[1], place.across_side()
+        else:
+            gains[1].wait_recv()
+            gain_total[2] = gain_total[1] + gain_parts[1]
+            source, target = gain_total.at[2, 1 - layer], place.across_layer()
+        part = gain_parts.at[position] if position < 2 else gain_parts.at[2, 0]
+        gains.append(push(source, part, gain_sent.at[position], gain_done.at[position], target))
+
+    def gain_last():
+        gains[2].wait_recv()
+        gain_total[0, 0] = gain_total[2, layer] + gain_parts[2, 0]
+        for step in range(1, DEPTHS):
+            gains.append(
+                push(
+                    gain_total.at[0, 0, place.other_depth(step)], gain_parts.at[2, 1, step],
+                    gain_sent.at[2 + step], gain_done.at[2 + step], place.along_depth(step),
+                )
+            )
+
+    def gain_finish():
+        value = gain_total[0, 0, depth]
+        for step in range(1, DEPTHS):
+            gains[2 + step].wait_recv()
+            value = value + gain_parts[2, 1, step]
+        gain_out[...] = value
+
+    place.greet()
+    ahead, gap = 3, 2
+    for unit in range(ahead):
+        begin(unit)
+    for step in range(UNITS + 3 * gap):
+        if step + ahead < UNITS:
+            begin(step + ahead)
+        if step < UNITS:
+            cross_first(step)
+        if 0 <= step - gap < UNITS:
+            cross_last(step - gap)
+        if 0 <= step - 2 * gap < UNITS:
+            along_depth(step - 2 * gap)
+        if 0 <= step - 3 * gap < UNITS:
+            finish(step - 3 * gap)
+        if step < 3:
+            gain_step(step)
+        elif step == 3:
+            gains[0].wait_send()
+            gain_last()
+        elif step == 4:
+            gain_finish()
+    for copy in cores + first + last + sum(deep, []) + gains[1:]:
+        copy.wait_send()
+
+
+def scatter_near(source_sums, target_sums):
+    dma = pltpu.SemaphoreType.DMA
+    vmem = pl.BlockSpec(memory_space=pltpu.VMEM)
+    shards = DEPTHS * SIDES * CORES
+    operands = []
+    for square, tall, gain in (source_sums, target_sums):
+        operands.append(square.reshape(BLOCKS, DEPTHS, SIDES, CORES, UNIT, D))
+        operands.append(tall.reshape(DEPTHS, SIDES, CORES, SLABS, UNIT, D))
+        operands.append(gain)
+    square, tall, gain = pl.pallas_call(
+        scatter_kernel,
+        in_specs=[ANYWHERE, ANYWHERE, vmem] * 2,
+        out_specs=[vmem] * 3,
+        out_shape=[shape_of((BLOCKS, UNIT, D), FULL), shape_of((SLABS * UNIT, D), FULL), shape_of((8, 128), FULL)],
+        scratch_shapes=[
+            pltpu.VMEM((UNITS, 2, DEPTHS, SIDES, UNIT, D), LOW),
+            pltpu.VMEM((UNITS, 2, DEPTHS, SIDES, UNIT, D), LOW),
+            pltpu.VMEM((UNITS, 2, DEPTHS, UNIT, D), LOW),
+            pltpu.VMEM((UNITS, DEPTHS, 2, UNIT, D), LOW),
+            pltpu.VMEM((UNITS, 2, DEPTHS, UNIT, D), LOW),
+            pltpu.VMEM((UNITS, DEPTHS, UNIT, D), LOW),
+            pltpu.VMEM((UNITS, DEPTHS, UNIT, D), LOW),
+            pltpu.VMEM((UNITS, 3, UNIT, D), LOW),
+            pltpu.VMEM((3, 2, DEPTHS, 8, 128), FULL),
+            pltpu.VMEM((3, 2, DEPTHS, 8, 128), FULL),
+            dma((UNITS, 2)), dma((UNITS, 2)), dma((UNITS, 2)), dma((UNITS,)), dma((UNITS,)), dma((UNITS,)),
+            dma((UNITS,)), dma((UNITS, 3)), dma((UNITS, 3)), dma((6,)), dma((6,)),
+        ],
+        compiler_params=pltpu.CompilerParams(
+            vmem_limit_bytes=VMEM_LIMIT, collective_id=1, has_side_effects=True
+        ),
+        name="scatter",
+    )(*operands)
+    start = lax.axis_index("dp") % 4 * UNIT
+    return square, tall, lax.dynamic_slice_in_dim(gain[:3], start, UNIT, axis=1)
+
+
+def scatter_sums(source_sums, target_sums, shards):
+    square, tall, gains = (jnp.stack(pair) for pair in zip(source_sums, target_sums))
     axes = ("pipe", "dp")
     square = jnp.swapaxes(square.reshape(2, BLOCKS, shards, D // shards, D), 1, 2)
-    gains = jnp.swapaxes(gains.reshape(2, 3, shards, D // shards), 1, 2)
+    gains = jnp.swapaxes(gains[:, :3].reshape(2, 3, shards, D // shards), 1, 2)
     square = square.reshape(2 * shards, BLOCKS, D // shards, D)
     tall = tall.reshape(2 * shards, FF // shards, D)
     gains = gains.reshape(2 * shards, 3, D // shards)
@@ -529,35 +923,36 @@
         return lax.dynamic_slice_in_dim(value, first, count, axis=0)
 
     mine = part(rows, start)
-    other = swap(part(rows, count - start))
+    source_counts = part(source_lengths, start)
+    target_counts = part(target_lengths, start)
+    shares = tuple(value[0] for value in (attention_in, attention_out, cross_weights, expand, contract))
+    if shards == DEPTHS * SIDES * CORES:
+        weights, other = gather_near(shares, norm_gains[0], rows)
+    else:
+        weights, other = gather_weights(shares, norm_gains[0], shards), swap(part(rows, count - start))
     source_rows = jnp.where(section == 0, mine, other)
     target_rows = jnp.where(section == 0, other, mine)
-    source_counts = part(source_lengths, start)
-    target_counts = part(target_lengths, start)
-
-    square = jnp.stack(
-        blocks_of(attention_in[0]) + [attention_out[0]] + blocks_of(cross_weights[0]) + blocks_of(expand[0])
-    ).astype(LOW)
-    weights = gather_weights(square, contract[0].astype(LOW), norm_gains[0], shards)
 
     memory, memory_pair, *kept = encode(source_counts, source_rows, weights)
-    output, target_gradient, delta_pair, *decoder_sums = decode(
+    output, target_gradient, delta_pair, *target_sums = decode(
         source_counts, target_counts, target_rows, memory_pair, part(cotangent, start), weights
     )
-    source_gradient, *encoder_sums = encode_back(source_rows, kept, delta_pair, weights)
-
-    def settle(source, target):
-        own = jnp.where(section == 0, source, target)
-        away = swap(jnp.where(section == 0, target, source).astype(LOW)).astype(FULL)
-        whole = jnp.zeros((2 * count, ROW, D), FULL)
-        whole = lax.dynamic_update_slice_in_dim(whole, own, start, axis=0)
-        return lax.dynamic_update_slice_in_dim(whole, away, count - start, axis=0)[None]
-
-    section_output = settle(memory, output)
-    input_gradient = settle(source_gradient, target_gradient)
-
-    square, tall, gains = (jnp.stack(pair) for pair in zip(encoder_sums, decoder_sums))
-    square, tall, gains = scatter_sums(square, tall, gains[:, :3], shards)
+    away_output = swap(jnp.where(section == 0, output, memory).astype(LOW))
+    away_target = lax.ppermute(target_gradient.astype(LOW), "pipe", [(0, 1)])
+    source_gradient, *source_sums = encode_back(source_rows, kept, delta_pair, weights)
+    away_source = lax.ppermute(source_gradient.astype(LOW), "pipe", [(1, 0)])
+    if shards == DEPTHS * SIDES * CORES:
+        square, tall, gains = scatter_near(source_sums, target_sums)
+    else:
+        square, tall, gains = scatter_sums(source_sums, target_sums, shards)
+
+    def settle(source, target, from_source, from_target):
+        upper = jnp.concatenate([source, from_source.astype(FULL)], axis=0)
+        lower = jnp.concatenate([from_target.astype(FULL), target], axis=0)
+        return jnp.where(section == 0, upper, lower)[None]
+
+    section_output = settle(memory, output, away_output, away_output)
+    input_gradient = settle(source_gradient, target_gradient, away_source, away_target)
 
     def joined(first, last):
         return jnp.concatenate([square[block] for block in range(first, last)], axis=1)[None]

time: 645 us -> 411 us (0.64)
  waiting for transfers between devices: 306 us -> 0.01 us
  Pallas kernels: 162 us -> 366 us
  blocking collectives: 80.9 us -> 0 us
  local copies, waits for them, and re-layouts: 34.3 us -> 8.65 us
  between operations: 14.2 us -> 1.05 us
  other arithmetic: 34.4 us -> 22.7 us
    pallas_call x0 -> x2, Pallas kernels: none -> 203 us  [the longest x1 110 us: gather_near(): pl.pallas_call(gather_kernel, in_specs=[vmem] * 6 + [ANYWHERE], out_specs...]
    reduce_scatter x2 -> x0, waiting for transfers between devices: 179 us -> none  [scatter_sums(): lax.psum_scatter(value, axes, scatter_dimension=0, tiled=False).astype(FULL)]
    all_gather x2 -> x0, waiting for transfers between devices: 92.8 us -> none  [the longest x1 53.9 us: gather_weights(): every_tall = lax.all_gather(tall, axes, axis=0, tiled=False)]
    all_gather x1 -> x0, blocking collectives: 40.9 us -> none  [gather_weights(): every_gain = lax.all_gather(gains.astype(LOW), axes, axis=0, tiled=False)]
    unnamed x1 -> x0, blocking collectives: 40 us -> none
    ppermute x3 -> x1, waiting for transfers between devices: 33.8 us -> 0.01 us  [swap(): return lax.ppermute(value, 'pipe', [(0, 1), (1, 0)])]
    transpose x1 -> x0, local copies, waits for them, and re-layouts: 10.2 us -> none  [scatter_sums(): jnp.swapaxes(square.reshape(2, BLOCKS, shards, D // shards, D), 1, 2)]
    reshape x3 -> x1, local copies, waits for them, and re-layouts: 10.3 us -> 0.61 us  [gather_near(): every_gain = jnp.swapaxes(every_gain, 1, 2).reshape(2, 3, D)]
  transfers between devices with their start and end apart: 7 -> 3, of which waited for: 6 -> 0; matrix products, arithmetic and copies ran while one was open for 9% -> 3% of each run, Pallas kernels for 0% -> 33%
where the time goes in v2:
time: 411 us; the launch traced here: 404 us
  Pallas kernels  366 us (89%)
  other arithmetic  22.7 us (6%)
  local copies, waits for them, and re-layouts  8.65 us (2%)
  starting transfers between devices  5.29 us (1%)
    pallas_call x1, Pallas kernels, gather_near(): pl.pallas_call(gather_kernel, in_specs=[vmem] * 6 + [ANYWHERE], out_specs...  110 us
    pallas_call x1, Pallas kernels, decode(): pl.pallas_call(decode_kernel, grid=(count,), in_specs=[SCALARS, SCALARS,...  98.2 us
    pallas_call x1, Pallas kernels, scatter_near(): pl.pallas_call(scatter_kernel, in_specs=[ANYWHERE, ANYWHERE, vmem] * 2, o...  93.1 us
    pallas_call x1, Pallas kernels, encode_back(): pl.pallas_call(encode_back_kernel, grid=(count,), in_specs=[per_row(ROW,...  40.5 us
    pallas_call x1, Pallas kernels, encode(): pl.pallas_call(encode_kernel, grid=(count,), in_specs=[SCALARS, per_row(R...  23.7 us
  transfers between devices with their start and end apart: 3, of which 0 were waited for; matrix products, arithmetic and copies ran while one was open for 3% of the time, Pallas kernels for 33%

profile of v2, /device:TPU:0, one launch (start us, length us, event | category | flops | bytes accessed | tf_op | source)
XLA Modules:
  0.0 403.6 jit_solution(11770195946868846763)
XLA Ops:
  0.7 0.7 convert_element_type.29
  1.4 0.1 tile.10
  1.5 0.6 pad.4.gains
  2.1 0.0 copy-start.7
  2.1 0.0 copy-start.8
  2.1 110.4 %gather.1 = (bf16[2,10,4,2,2,32,512]{6,5,4,3,2,1,0:T(8,128)(2,1)}, bf16[2,4,2,2,4,32,512]{6,5,4,3,2,1,0:T(8,128)(2,1)}, bf16[2,4,2,2,16,128]{5,4,3,2,1,0:T(8,128)(2,1)}, bf16[2,512,512]{2,1,0:T(8,128)(2,1)}) custom-call(f32[32,1536]{1,0:T(8,128)} %bitcast.80, f32[32,512]{1,0:T(8,128)} %bitcast.82, f32[32,1024]{1,0:T(8,128)} %bitcast.81, ...), custom_call_target="tpu_custom_call" | custom-call | tf_op jit(solution)/shard_map/gather/pallas_call | solution.py:646
  112.4 0.0 copy-start.5
  112.4 1.1 convert_reduce_fusion
  113.5 0.6 slice_bitcast_fusion.9.gains
  114.1 2.3 constant_dynamic-slice_fusion.cotangent
  116.4 0.0 copy-done.7
  116.4 0.0 copy-done.8
  116.4 0.6 constant_dynamic-slice_fusion.1
  117.0 0.0 copy-done.5
  117.0 2.7 bitcast_select_fusion.1
  119.7 23.7 %encode.1 = (f32[2,512,512]{2,1,0:T(8,128)}, bf16[2,512,1024]{2,1,0:T(8,128)(2,1)}, bf16[2,512,1536]{2,1,0:T(8,128)(2,1)}, bf16[2,8,512,512]{3,2,1,0:T(8,128)(2,...) custom-call(s32[2,4]{1,0:T(2,128)} %get-tuple-element.101.source_cou, ...), custom_call_target="tpu_custom_call" | custom-call | tf_op jit(solution)/shard_map/encode/pallas_call | solution.py:408
  143.4 98.2 %decode.1 = (f32[2,512,512]{2,1,0:T(8,128)}, f32[2,512,512]{2,1,0:T(8,128)}, bf16[2,512,1024]{2,1,0:T(8,128)(2,1)}, bf16[10,512,512]{2,1,0:T(8,128)(2,1)}, bf16[2048,512]{1,0:T(8,128)(2,1)}, /*index=5*/f32[8,512]{1,0:T(8,128)}) custom-call(s32[2,4]{1,0:T(2,128)} %get-tuple-element.101.source_counts, s32[2,4]{1,0:T(2,128)} %get-tuple-element.100.target_counts, ...), custom_call_target="tpu_custom_call" | custom-call | tf_op jit(solution)/shard_map/decode/pallas_call | solution.py:428
  241.6 0.0 copy-start
  241.6 3.1 select_convert_fusion
  244.7 0.6 collective-permute-start
  245.3 0.0 copy-done
  245.3 1.1 convert_element_type.34
  246.4 3.5 collective-permute-start.2
  249.8 40.5 %encode_back.1 = (f32[2,512,512]{2,1,0:T(8,128)}, bf16[10,512,512]{2,1,0:T(8,128)(2,1)}, bf16[2048,512]{1,0:T(8,128)(2,1)}, f32[8,512]{1,0:T(8,128)}) custom-call(bf16[2,512,512]{2,1,0:T(8,128)(2,1)} %get-tuple-element.86.rows, bf16[2,8,512,512]{3,2,1,0:T(8,128)(2,1)} %get-tuple-element.42.shares_in, bf16[2,512,1536]{2,1,0:T(8,128)(2,1)} %get-tuple-element.43.triple, ...), custom_call_target="tpu_custom_call" | custom-call | tf_op jit(solution)/shard_map/encode_back/pallas_call | solution.py:453
  290.4 2.7 convert_element_type.33
  293.1 1.3 collective-permute-start.1
  294.4 93.1 %scatter.1 = (f32[10,32,512]{2,1,0:T(8,128)}, f32[128,512]{1,0:T(8,128)}, f32[8,128]{1,0:T(8,128)}) custom-call(bf16[10,4,2,2,32,512]{5,4,3,2,1,0:T(8,128)(2,1)} %bitcast.73, bf16[4,2,2,4,32,512]{5,4,3,2,1,0:T(8,128)(2,1)} %bitcast.76, f32[8,512]{1,0:T(8,128)} %get-tuple-element.55.source_gain, bf16[10,4,2,2,32,512]{5,4,3,2,1,0:T(8,128)(2,1)} %bitcast.72, ...), custom_call_target="tpu_custom_call" | custom-call | tf_op jit(solution)/shard_map/scatter/pallas_call | solution.py:854
  387.5 0.7 slice.47
  388.2 0.1 dynamic-slice_bitcast_fusion
  388.2 0.6 copy.27
  388.8 1.8 slice_bitcast_fusion.3
  390.6 0.0 copy-start.4
  390.6 0.7 maximum_bitcast_fusion.2
  391.3 0.0 copy-start.3
  391.3 0.7 maximum_bitcast_fusion.1
  392.0 0.7 maximum_bitcast_fusion
  392.7 0.0 collective-permute-done
  392.7 1.5 bitcast_convert_fusion.2
  394.2 0.0 copy-done.4
  394.2 0.0 copy-done.3
  394.2 2.8 maximum_select_fusion
  397.0 0.0 collective-permute-done.2
  397.0 0.0 copy-start.2
  397.0 0.3 bitcast_convert_fusion
  397.3 0.0 copy-start.1
  397.3 0.0 collective-permute-done.1
  397.3 1.6 bitcast_convert_fusion.1
  398.9 0.0 copy-done.2
  399.0 0.6 copy-done.1
  399.6 0.0 copy-start.6
  399.6 3.0 maximum_select_fusion.1
  402.6 0.0 copy-done.6
  402.6 0.7 copy.32
  (5 shorter events, 0.0 us)
Async XLA Ops:
  2.1 114.3 %copy-start.7 = (s32[4,4]{1,0:T(4,128)S(1)}, s32[4,4]{1,0:T(4,128)}, u32[]{:S(2)}) copy-start(s32[4,4]{1,0:T(4,128)} %param.18) | copy-start | bytes 196
  2.1 114.3 %copy-start.8 = (s32[4,4]{1,0:T(4,128)S(1)}, s32[4,4]{1,0:T(4,128)}, u32[]{:S(2)}) copy-start(s32[4,4]{1,0:T(4,128)} %param.17) | copy-start | bytes 196
  112.4 4.5 %copy-start.5 = (bf16[1,4,512,512]{3,2,1,0:T(8,128)(2,1)S(1)}, bf16[1,4,512,512]{3,2,1,0:T(8,128)(2,1)}, u32[]{:S(2)}) copy-start(bf16[1,4,512,512]{3,2,1,0:T(8,128)(2,1)} %param.10) | copy-start | bytes 6291460
  241.6 3.7 copy-start
  244.7 147.9 %collective-permute-start = (bf16[2,512,512]{2,1,0:T(8,128)(2,1)}, bf16[2,512,512]{2,1,0:T(8,128)(2,1)}, u32[]{:S(2)}, u32[]{:S(2)}) collective-permute-start(bf16[2,512,512]{2,1,0:T(8,128)(2,1)} %select_convert_fusion), channel_id=1, source_target_pairs={{0,16},{16,0},{1,17},{17,1},{2,18},{18,2},{3,19},{19,3},{4,20},{20... | collective-permute-start | bytes 3145736 | tf_op jit(solution)/shard_map/ppermute | solution.py:897
  246.4 150.6 %collective-permute-start.2 = (bf16[2,512,512]{2,1,0:T(8,128)(2,1)}, bf16[2,512,512]{2,1,0:T(8,128)(2,1)S(1)}, u32[]{:S(2)}, u32[]{:S(2)}) collective-permute-start(bf16[2,512,512]{2,1,0:T(8,128)(2,1)} %convert_element_type.34), channel_id=1, source_target_pairs={{0,16},{1,17},{2,18},{3,19},{4,20},{5,21},{6,22},{7,23},{8,24},{9,... | collective-permute-start | bytes 3145736 | tf_op jit(solution)/shard_map/ppermute | solution.py:941
  293.1 104.2 %collective-permute-start.1 = (bf16[2,512,512]{2,1,0:T(8,128)(2,1)}, bf16[2,512,512]{2,1,0:T(8,128)(2,1)}, u32[]{:S(2)}, u32[]{:S(2)}) collective-permute-start(bf16[2,512,512]{2,1,0:T(8,128)(2,1)} %convert_element_type.33), channel_id=1, source_target_pairs={{16,0},{17,1},{18,2},{19,3},{20,4},{21,5},{22,6},{23,7},{24,8},{25... | collective-permute-start | bytes 3145736 | tf_op jit(solution)/shard_map/ppermute | solution.py:943
  390.6 3.6 copy-start.4
  391.3 2.9 copy-start.3
  397.0 2.0 copy-start.2
  397.3 2.3 copy-start.1
  399.6 3.0 copy-start.6

commit v3 on v1

v3 whole, which is shorter than its diff:
```python
from functools import partial
import math

import jax
import jax.numpy as jnp
from jax import lax
from jax.experimental import pallas as pl
from jax.experimental.pallas import tpu as pltpu
from jax.sharding import PartitionSpec as P

D = 512
HEADS = 8
HD = 64
FF = 2048
ROW = 512
PAIRS = HEADS // 2
PACK = 4

QKV, OUT, SELFS = 0, 3, 4
CROSS, EXPAND, BLOCKS = 0, 2, 6
SLABS = FF // D
UNITS = BLOCKS + SLABS

EPSILON = 1e-05
MASKED = -1e30
LOG2E = math.log2(math.e)
EXPONENT = HD**-0.5 * LOG2E
BELL = 1.0 / math.sqrt(2.0 * math.pi)
LOW = jnp.bfloat16
FULL = jnp.float32
VMEM_LIMIT = 63 * 2**20

NN = (((1,), (0,)), ((), ()))
NT = (((1,), (1,)), ((), ()))
TN = (((0,), (0,)), ((), ()))


def multiply(left, right, dims=NN):
    return lax.dot_general(left, right, dims, preferred_element_type=jnp.float32)


def columns(index, width=D):
    return pl.ds(index * width, width)


def normalize(stream):
    centred = stream - jnp.mean(stream, axis=1, keepdims=True)
    scale = lax.rsqrt(jnp.mean(centred * centred, axis=1, keepdims=True) + EPSILON)
    return centred * scale, scale


def norm_back(unit, scale, gain, delta):
    inner = delta * gain
    mean = jnp.mean(inner, axis=1, keepdims=True)
    along = jnp.mean(inner * unit, axis=1, keepdims=True)
    return scale * (inner - mean - unit * along), jnp.sum(delta * unit, axis=0, keepdims=True)


def segment(counts, shape, axis):
    places = lax.broadcasted_iota(jnp.int32, shape, axis)
    end = counts[0]
    found = (places >= end).astype(jnp.int32)
    for count in counts[1:]:
        end = end + count
        found = found + (places >= end).astype(jnp.int32)
    return found


def segments(counts):
    return segment(counts, (ROW, 1), 0), segment(counts, (1, ROW), 1)


def fill_bias(bias, query_segment, key_segment, causal=None):
    keep = query_segment == key_segment
    if causal is not None:
        query = lax.broadcasted_iota(jnp.int32, (ROW, ROW), 0)
        key = lax.broadcasted_iota(jnp.int32, (ROW, ROW), 1)
        keep = keep & (key <= query + jnp.where(causal, 0, ROW))
    bias[...] = jnp.where(keep, 0.0, MASKED).astype(bias.dtype)


def lanes():
    return lax.broadcasted_iota(jnp.int32, (1, 2 * HD), 1)


def only_half(value, half):
    return jnp.where(lanes() // HD == half, value, jnp.zeros_like(value))


def attend(query, keys, values, bias, shares, inverse, result, hook):
    kept = jnp.zeros((ROW, 2 * HD), FULL)
    for pair in range(PAIRS):
        query2, keys2, values2 = query(pair), keys(pair), values(pair)
        parts = []
        for half in range(2):
            head = 2 * pair + half
            scores = multiply(only_half(query2, half), keys2, NT) + bias[...]
            top = jnp.max(scores, axis=1, keepdims=True)
            weights = jnp.exp2((scores - top) * EXPONENT)
            scale = 1.0 / jnp.sum(weights, axis=1, keepdims=True)
            low = weights.astype(LOW)
            shares[head] = low
            parts.append(multiply(low, values2) * scale)
            kept = jnp.where(lanes() == head, scale, kept)
        result[:, columns(pair, 2 * HD)] = jnp.where(lanes() < HD, parts[0], parts[1]).astype(LOW)
        hook()
    inverse[...] = kept


def attend_back(query, keys, values, shares, inverse, result, delta, put, hook):
    for pair in range(PAIRS):
        query2, keys2, values2 = query(pair), keys(pair), values(pair)
        place = slice(2 * HD * pair, 2 * HD * (pair + 1))
        scale = jnp.where(
            lanes() < HD, inverse[:, 2 * pair : 2 * pair + 1], inverse[:, 2 * pair + 1 : 2 * pair + 2]
        )
        low = (delta[:, place] * scale).astype(LOW)
        product = low.astype(FULL) * result[:, columns(pair, 2 * HD)].astype(FULL)
        query_turned, low_turned = query2.T, low.T
        delta_query = 0.0
        delta_keys, delta_values = [], []
        for half in range(2):
            weights = shares[2 * pair + half]
            along = jnp.sum(only_half(product, half), axis=1, keepdims=True)
            delta_shares = multiply(only_half(low, half), values2, NT)
            delta_scores = (weights.astype(FULL) * (delta_shares - along)).astype(LOW)
            delta_query = delta_query + multiply(delta_scores, only_half(keys2, half))
            own = slice(HD * half, HD * (half + 1))
            delta_keys.append(multiply(query_turned[own], delta_scores))
            delta_values.append(multiply(low_turned[own], weights))
        keys_turned = (jnp.concatenate(delta_keys, axis=0) * HD**-0.5).astype(LOW)
        values_turned = jnp.concatenate(delta_values, axis=0).astype(LOW)
        put(pair, (delta_query * HD**-0.5).astype(LOW), keys_turned.T, values_turned.T)
        hook()


def self_parts(triple):
    return tuple(
        (lambda pair, start=part * PAIRS: triple[:, columns(start + pair, 2 * HD)]) for part in range(3)
    )


def put_triple(target):
    def put(pair, *parts):
        for part, value in enumerate(parts):
            target[:, columns(part * PAIRS + pair, 2 * HD)] = value

    return put


def feed(normed, stream, square, tall, active, slope):
    total = stream
    for slab in range(SLABS):
        hidden = multiply(normed, square[EXPAND + slab])
        under = 0.5 + 0.5 * lax.erf(hidden * math.sqrt(0.5))
        bell = BELL * jnp.exp2(hidden * hidden * (-0.5 * LOG2E))
        low = (hidden * under).astype(LOW)
        active[:, columns(slab)] = low
        slope[:, columns(slab)] = (under + hidden * bell).astype(LOW)
        total = total + multiply(low, tall[columns(slab), :])
    return total


def feed_back(delta, stream, gain, square, tall, change):
    unit, scale = normalize(stream)
    low = delta.astype(LOW)
    delta_normed = 0.0
    for slab in range(SLABS):
        delta_active = multiply(low, tall[columns(slab), :], NT)
        delta_hidden = (delta_active * change[:, columns(slab)].astype(FULL)).astype(LOW)
        change[:, columns(slab)] = delta_hidden
        delta_normed = delta_normed + multiply(delta_hidden, square[EXPAND + slab], NT)
    delta_stream, delta_gain = norm_back(unit, scale, gain, delta_normed)
    return delta + delta_stream, delta_gain


def self_forward(stream, gain, square, bias, triple, shares, inverse, result, hook):
    normed = (normalize(stream)[0] * gain).astype(LOW)
    for part in range(3):
        triple[:, columns(part)] = multiply(normed, square(QKV + part)).astype(LOW)
    hook()
    attend(*self_parts(triple), bias, shares, inverse, result, hook)
    return stream + multiply(result[...], square(OUT))


def self_back(low, stream, gain, square, triple, shares, inverse, result, delta_triple, sums, hook):
    unit, scale = normalize(stream)
    sums[OUT] += multiply(result[...], low, TN)
    delta_result = multiply(low, square(OUT), NT)
    hook()
    attend_back(*self_parts(triple), shares, inverse, result, delta_result, put_triple(delta_triple), hook)
    turned = (unit * gain).astype(LOW).T
    delta_normed = 0.0
    for part in range(3):
        chunk = delta_triple[:, columns(part)]
        sums[QKV + part] += multiply(turned, chunk)
        delta_normed = delta_normed + multiply(chunk, square(QKV + part), NT)
    delta_stream, delta_gain = norm_back(unit, scale, gain, delta_normed)
    return low.astype(FULL) + delta_stream, delta_gain


def middle_kernel(
    source_counts, target_counts, first, away, cotangent, square, tall, gains,
    section_output, sent_output, kept_delta, sent_delta, square_out, tall_out, gain_out,
    bias, shares, inverse, cross_result, source_end, target_mid, value,
    source_normed, source_active, memory_low, cross_normed, feed_normed, target_active,
    source_change, source_low, delta_pair, delta_question, cross_low, target_change, target_low,
    gain_sum, loaded, stored, ready,
):
    step = pl.program_id(0)
    layer = lax.axis_index("pipe")
    count = loaded.shape[0]
    source_square, target_square = square.at[0], square.at[1]
    source_tall, target_tall = tall.at[0], tall.at[1]

    def load(row):
        return pltpu.make_async_copy(
            cotangent.at[layer * count + row], target_low.at[columns(row, ROW), :], loaded.at[row]
        )

    def store(row):
        return pltpu.make_async_copy(value, section_output.at[layer * count + row], stored)

    @pl.when(step == 0)
    def _():
        gain_sum[...] = jnp.zeros(gain_sum.shape, FULL)
        for row in range(loaded.shape[0]):
            load(row).start()

    @pl.when(step < count)
    def _():
        row = step
        place = pl.ds(pl.multiple_of(row * ROW, ROW), ROW)
        own, other = first[0], away[0].astype(FULL)
        source_stream = jnp.where(layer == 0, own, other)
        target_stream = jnp.where(layer == 0, other, own)
        whole = layer * count + row
        source_segment = segments([source_counts[whole, piece] for piece in range(PACK)])
        target_segment = segments([target_counts[whole, piece] for piece in range(PACK)])

        unit, _ = normalize(source_stream)
        normed = (unit * gains[0, 1:2, :]).astype(LOW)
        source_normed[place, :] = normed
        end = feed(
            normed, source_stream, source_square, source_tall, source_active.at[place, :], source_change.at[place, :]
        )
        source_end[...] = end
        memory = normalize(end)[0] * gains[0, 2:3, :]
        low = memory.astype(LOW)
        memory_low[place, :] = low
        for part in range(2):
            delta_pair[place, columns(part)] = multiply(low, source_square[CROSS + part]).astype(LOW)

        fill_bias(bias, target_segment[0], source_segment[1])
        unit, _ = normalize(target_stream)
        normed = (unit * gains[1, 1:2, :]).astype(LOW)
        cross_normed[place, :] = normed
        delta_question[place, :] = multiply(normed, target_square[CROSS]).astype(LOW)
        cross = (
            lambda pair: delta_question[place, columns(pair, 2 * HD)],
            lambda pair: delta_pair[place, columns(pair, 2 * HD)],
            lambda pair: delta_pair[place, columns(PAIRS + pair, 2 * HD)],
        )
        result = cross_result.at[place, :]
        attend(*cross, bias, shares, inverse, result, no_hook)
        stream = target_stream + multiply(result[...], target_square[CROSS + 1])
        target_mid[...] = stream
        normed = (normalize(stream)[0] * gains[1, 2:3, :]).astype(LOW)
        feed_normed[place, :] = normed
        output = feed(
            normed, stream, target_square, target_tall, target_active.at[place, :], target_change.at[place, :]
        )

        @pl.when(row > 0)
        def _():
            store(row).wait()

        value[...] = jnp.where(layer == 0, memory, output)
        store(row).start()
        sent_output[0] = jnp.where(layer == 0, output, memory).astype(LOW)

        load(row).wait()
        delta, delta_gain = feed_back(
            target_low[place, :].astype(FULL), target_mid[...], gains[1, 2:3, :], target_square, target_tall,
            target_change.at[place, :],
        )
        gain_sum[1, 2:3, :] += delta_gain

        unit, scale = normalize(target_stream)
        low = delta.astype(LOW)
        cross_low[place, :] = low
        delta_result = multiply(low, target_square[CROSS + 1], NT)

        def put(pair, query, keys, values):
            delta_question[place, columns(pair, 2 * HD)] = query
            delta_pair[place, columns(pair, 2 * HD)] = keys
            delta_pair[place, columns(PAIRS + pair, 2 * HD)] = values

        attend_back(*cross, shares, inverse, result, delta_result, put, no_hook)
        delta_normed = multiply(delta_question[place, :], target_square[CROSS], NT)
        delta_stream, delta_gain = norm_back(unit, scale, gains[1, 1:2, :], delta_normed)
        gain_sum[1, 1:2, :] += delta_gain
        target_delta = (delta + delta_stream).astype(LOW)

        unit, scale = normalize(source_end[...])
        delta_memory = 0.0
        for part in range(2):
            delta_memory = delta_memory + multiply(delta_pair[place, columns(part)], source_square[CROSS + part], NT)
        delta, delta_gain = norm_back(unit, scale, gains[0, 2:3, :], delta_memory)
        gain_sum[0, 2:3, :] += delta_gain
        source_low[place, :] = delta.astype(LOW)
        delta, delta_gain = feed_back(
            delta, source_stream, gains[0, 1:2, :], source_square, source_tall, source_change.at[place, :]
        )
        gain_sum[0, 1:2, :] += delta_gain
        source_delta = delta.astype(LOW)
        kept_delta[0] = jnp.where(layer == 0, source_delta, target_delta)
        sent_delta[0] = jnp.where(layer == 0, target_delta, source_delta)

    @pl.when(step == count)
    def _():
        store(0).wait()
        gain_out[...] = gain_sum[...]
        copies = []

        def emit(result, target):
            slot = len(copies) % HEADS
            if len(copies) >= HEADS:
                copies[len(copies) - HEADS].wait()
            shares[slot] = result.astype(LOW)
            copy = pltpu.make_async_copy(shares.at[slot], target, ready.at[slot])
            copy.start()
            copies.append(copy)

        for which, normed, change, active, low in (
            (1, feed_normed, target_change, target_active, target_low),
            (0, source_normed, source_change, source_active, source_low),
        ):
            turned = normed[...].T
            for slab in range(SLABS):
                emit(multiply(turned, change[:, columns(slab)]), square_out.at[which, EXPAND + slab])
            for slab in range(SLABS):
                emit(multiply(active[:, columns(slab)], low[...], TN), tall_out.at[which, columns(slab), :])
        emit(multiply(cross_normed[...], delta_question[...], TN), square_out.at[1, CROSS])
        emit(multiply(cross_result[...], cross_low[...], TN), square_out.at[1, CROSS + 1])
        turned = memory_low[...].T
        for part in range(2):
            emit(multiply(turned, delta_pair[:, columns(part)]), square_out.at[0, CROSS + part])
        for copy in copies[-HEADS:]:
            copy.wait()


def no_hook():
    pass


def per_row(*shape, last=None, start=0, buffers=2):
    def index(row):
        return (start + (row if last is None else jnp.minimum(row, last)),) + (0,) * len(shape)

    return pl.BlockSpec((1,) + shape, index, pipeline_mode=pl.Buffered(buffers) if buffers != 2 else None)


def constant(*shape):
    return pl.BlockSpec(shape, lambda row: (0,) * len(shape), pipeline_mode=pl.Buffered(1))


ANYWHERE = pl.BlockSpec(memory_space=pl.ANY)
SCALARS = pl.BlockSpec(memory_space=pltpu.SMEM)
PARAMS = pltpu.CompilerParams(vmem_limit_bytes=VMEM_LIMIT)


def shape_of(shape, kind):
    return jax.ShapeDtypeStruct(shape, kind)


def middle(source_counts, target_counts, first, away, cotangent, square, tall, gains):
    count = away.shape[0]
    tokens = count * ROW
    full = pltpu.VMEM((ROW, D), FULL)
    kept, pair, wide = (pltpu.VMEM((tokens, width), LOW) for width in (D, 2 * D, FF))
    last = count - 1
    return pl.pallas_call(
        middle_kernel,
        grid=(count + 1,),
        in_specs=[
            SCALARS, SCALARS, per_row(ROW, D, last=last, start=count, buffers=1),
            per_row(ROW, D, last=last, buffers=1), ANYWHERE,
            constant(2, BLOCKS, D, D), constant(2, FF, D), constant(2, 8, D),
        ],
        out_specs=[ANYWHERE]
        + [per_row(ROW, D, last=last)] * 3
        + [ANYWHERE, ANYWHERE, pl.BlockSpec((2, 8, D), lambda row: (0, 0, 0))],
        out_shape=[shape_of((2 * count, ROW, D), FULL)]
        + [shape_of((count, ROW, D), LOW)] * 3
        + [shape_of((2, BLOCKS, D, D), LOW), shape_of((2, FF, D), LOW), shape_of((2, 8, D), FULL)],
        scratch_shapes=[
            pltpu.VMEM((ROW, ROW), LOW), pltpu.VMEM((HEADS, ROW, ROW), LOW),
            pltpu.VMEM((ROW, 2 * HD), FULL), kept, full, full, full,
            kept, wide, kept, kept, kept, wide,
            wide, kept, pair, kept, kept, wide, kept,
            pltpu.VMEM((2, 8, D), FULL), pltpu.SemaphoreType.DMA((count,)), pltpu.SemaphoreType.DMA,
            pltpu.SemaphoreType.DMA((HEADS,)),
        ],
        compiler_params=PARAMS,
        name="middle",
    )(source_counts, target_counts, first, away, cotangent, square, tall, gains)


MESH = pl.DeviceIdType.MESH
UNITS = BLOCKS + SLABS
UNIT = 32
DEPTHS, SIDES, CORES = 4, 2, 2


class Place:
    def __init__(self):
        self.layer = lax.axis_index("pipe")
        self.rank = lax.axis_index("dp")
        self.core = self.rank % CORES
        self.side = self.rank // CORES % SIDES
        self.depth = self.rank // (CORES * SIDES)

    def sibling(self):
        return (self.layer, self.rank + 1 - 2 * self.core)

    def across_side(self):
        return (self.layer, self.rank + CORES * (1 - 2 * self.side))

    def across_layer(self):
        return (1 - self.layer, self.rank)

    def other_depth(self, step):
        return (self.depth + step) % DEPTHS

    def along_depth(self, step):
        return (self.layer, self.rank + CORES * SIDES * (self.other_depth(step) - self.depth))

    def greet(self):
        partners = [self.sibling(), self.across_side(), self.across_layer()]
        partners += [self.along_depth(step) for step in range(1, DEPTHS)]
        barrier = pltpu.get_barrier_semaphore()
        for partner in partners:
            pl.semaphore_signal(barrier, inc=1, device_id=partner, device_id_type=MESH)
        pl.semaphore_wait(barrier, len(partners))


def layer_first(unit):
    return unit % 4 != 3


def row_of(layer, slot, count):
    return (slot + count * (1 - layer)) % (2 * count)


class Plan:
    def __init__(self, rate, hooks):
        self.rate, self.hooks = rate, hooks
        self.steps = {}
        self.index = 0

    def fill(self, thunks, rows):
        for number, thunk in enumerate(thunks):
            place = min(int(number * self.rate), rows * self.hooks - 1)
            self.steps.setdefault(divmod(place, self.hooks), []).append(thunk)

    def hook(self):
        index, self.index = self.index, self.index + 1
        step = pl.program_id(0)
        for (row, place), thunks in sorted(self.steps.items(), key=lambda item: item[0]):
            if place == index:

                @pl.when(step == row)
                def _(thunks=thunks):
                    for thunk in thunks:
                        thunk()


class Copies:
    def __init__(self):
        self.made = {}

    def define(self, key, parts):
        def make():
            source, target, sent, arrived, device = parts()
            return pltpu.make_async_remote_copy(
                src_ref=source, dst_ref=target, send_sem=sent, recv_sem=arrived, device_id=device,
                device_id_type=MESH,
            )

        self.made[key] = make

    def start(self, *keys):
        for key in keys:
            self.made[key]().start()

    def arrived(self, *keys):
        for key in keys:
            self.made[key]().wait_recv()

    def finish(self):
        for make in self.made.values():
            make().wait_send()


GATHER_RATE, GATHER_AHEAD, GATHER_GAP = 1.5, 4, 2
SCATTER_RATE, SCATTER_AHEAD, SCATTER_GAP = 1.4, 3, 2
ORDER = (2, 3, 4, 5, 6, 7, 8, 9, 0, 1)
HOOKS = PAIRS + 2


def near_self_kernel(
    source_counts, target_counts, attention_in, attention_out, cross, expand, contract, gains, rows,
    square, tall, own_square, every_gain, away, triple, shares, inverse, result, first,
    blocks, tiles, streams, sending, bias, own,
    own_done, fetched, block_sent, block_done, block_out, tile_sent, tile_done,
    depth_sent, depth_done, first_sent, first_done, last_sent, last_done, core_sent, core_done,
    away_sent, away_done,
):
    place = Place()
    layer, depth, side, core = place.layer, place.depth, place.side, place.core
    step, total = pl.program_id(0), 2 * away.shape[0]
    count = away.shape[0]
    everything = slice(None)
    copies = Copies()
    selfs = [attention_in.at[:, columns(j)] for j in range(3)] + [attention_out]
    sources = [cross.at[:, columns(j)] for j in range(2)] + [expand.at[:, columns(j)] for j in range(SLABS)]
    sources += [contract.at[columns(j, UNIT), :] for j in range(SLABS)]

    def spot(unit, *index):
        if unit < BLOCKS:
            return square.at[(index[0], unit) + index[1:]]
        return tall.at[index + (unit - BLOCKS,)]

    def from_layers(unit):
        return spot(unit, everything, everything, side, core)

    def from_sides(unit):
        return spot(unit, layer, everything, everything, core)

    def deep_parts(unit, away_by):
        slot = (unit, away_by - 1)
        target = spot(unit, layer, depth, side, core)
        return own.at[unit], target, depth_sent.at[slot], depth_done.at[slot], place.along_depth(away_by)

    def first_parts(unit):
        block = spot(unit, layer, everything, side, core)
        target = place.across_layer() if layer_first(unit) else place.across_side()
        return block, block, first_sent.at[unit], first_done.at[unit], target

    def last_parts(unit):
        if layer_first(unit):
            block, target = from_layers(unit), place.across_side()
        else:
            block, target = from_sides(unit), place.across_layer()
        return block, block, last_sent.at[unit], last_done.at[unit], target

    def core_parts(unit):
        block = spot(unit, everything, everything, everything, core)
        return block, block, core_sent.at[unit], core_done.at[unit], place.sibling()

    for unit in range(UNITS):
        for away_by in range(1, DEPTHS):
            copies.define(("deep", unit, away_by), partial(deep_parts, unit, away_by))
        copies.define(("first", unit), partial(first_parts, unit))
        copies.define(("last", unit), partial(last_parts, unit))
        copies.define(("core", unit), partial(core_parts, unit))

    def away_parts(slot):
        return sending.at[slot], away.at[slot], away_sent.at[slot], away_done.at[slot], place.across_layer()

    def block_parts(unit, stage):
        if stage == 0:
            block, target = blocks.at[unit, :, :, core], place.sibling()
        elif stage < DEPTHS:
            block, target = blocks.at[unit, depth, side, core], place.along_depth(stage)
        else:
            block, target = blocks.at[unit, :, side, core], place.across_side()
        return block, block, block_sent.at[unit, stage], block_done.at[unit, stage], target

    def tile_parts(stage):
        if stage == 0:
            block, target = tiles.at[layer], place.across_layer()
        elif stage < DEPTHS:
            block, target = tiles.at[layer, depth, side, core], place.along_depth(stage)
        elif stage == DEPTHS:
            block, target = tiles.at[layer, :, side, core], place.across_side()
        else:
            block, target = tiles.at[layer, :, :, core], place.sibling()
        return block, block, tile_sent.at[stage], tile_done.at[stage], target

    for stage in range(DEPTHS + 2):
        copies.define(("tile", stage), partial(tile_parts, stage))
    for unit in range(SELFS):
        for stage in range(DEPTHS + 1):
            copies.define(("block", unit, stage), partial(block_parts, unit, stage))
    for slot in range(count):
        copies.define(("away", slot), partial(away_parts, slot))

    def keep(unit):
        return pltpu.make_async_copy(own.at[unit], spot(unit, layer, depth, side, core), own_done.at[unit])

    def deep(unit):
        return [("deep", unit, away_by) for away_by in range(1, DEPTHS)]

    def begin(unit):
        own[unit] = sources[unit][...].astype(LOW)
        keep(unit).start()
        copies.start(*deep(unit))

    def cross_first(unit):
        keep(unit).wait()
        copies.arrived(*deep(unit))
        copies.start(("first", unit))

    def cross_last(unit):
        copies.arrived(("first", unit))
        copies.start(("last", unit))

    def share(unit):
        copies.arrived(("last", unit))
        copies.start(("core", unit))

    def steps():
        gap, ahead = GATHER_GAP, GATHER_AHEAD

        def one(number):
            if ahead <= number + ahead < UNITS:
                begin(ORDER[number + ahead])
            if number < UNITS:
                cross_first(ORDER[number])
            if 0 <= number - gap < UNITS:
                cross_last(ORDER[number - gap])
            if 0 <= number - 2 * gap < UNITS:
                share(ORDER[number - 2 * gap])

        return [partial(one, number) for number in range(UNITS + 2 * gap)]

    def lay_gains(which):
        for row in range(DEPTHS):
            value = tiles[which, row, 0, 0].astype(FULL)
            for other in ((0, 1), (1, 0), (1, 1)):
                value = value + tiles[(which, row) + other].astype(FULL)
            every_gain[which, :, columns(row, 128)] = value[:8]

    def fetch(slot):
        return pltpu.make_async_copy(
            rows.at[row_of(layer, slot, count)], streams.at[slot % 2], fetched.at[slot % 2]
        )

    @pl.when(step == 0)
    def _():
        fetch(step).start()
        for unit in range(SELFS):
            blocks[unit, depth, side, core] = selfs[unit][...].astype(LOW)
        tiles[layer, depth, side, core] = gains[...]
        place.greet()
        across = range(1, DEPTHS)
        copies.start(*[("tile", stage) for stage in across])
        for unit in range(SELFS):
            copies.start(*[("block", unit, stage) for stage in across])
        for number in range(GATHER_AHEAD):
            begin(ORDER[number])
        copies.arrived(*[("tile", stage) for stage in across])
        copies.start(("tile", DEPTHS))
        for unit in range(SELFS):
            copies.arrived(*[("block", unit, stage) for stage in across])
            copies.start(("block", unit, DEPTHS))
        copies.arrived(("tile", DEPTHS))
        copies.start(("tile", DEPTHS + 1))
        for unit in range(SELFS):
            copies.arrived(("block", unit, DEPTHS))
            copies.start(("block", unit, 0))
        copies.arrived(("tile", DEPTHS + 1))
        copies.start(("tile", 0))
        lay_gains(layer)
        copies.arrived(*[("block", unit, 0) for unit in range(SELFS)])
        pltpu.make_async_copy(blocks, own_square, block_out).start()

    plan = Plan(GATHER_RATE, HOOKS)
    plan.fill(steps(), total)

    @pl.when(step + 1 < total)
    def _():
        fetch(step + 1).start()

    row = row_of(layer, step, count)
    causal = layer == 1
    both = [jnp.where(causal, target_counts[row, piece], source_counts[row, piece]) for piece in range(PACK)]
    fill_bias(bias, *segments(both), causal)
    fetch(step).wait()
    stream = self_forward(
        streams[step % 2].astype(FULL), every_gain[layer, 0:1, :], lambda unit: blocks[unit].reshape(D, D), bias,
        triple.at[0], shares.at[0], inverse.at[0], result.at[0], plan.hook,
    )
    first[0] = stream

    for slot in range(count):

        @pl.when(step == slot)
        def _(slot=slot):
            sending[slot] = stream.astype(LOW)
            copies.start(("away", slot))

    plan.hook()

    @pl.when(step == total - 1)
    def _():
        copies.arrived(("tile", 0))
        lay_gains(1 - layer)
        copies.arrived(*[("core", unit) for unit in range(UNITS)])
        copies.arrived(*[("away", slot) for slot in range(count)])
        copies.finish()
        pltpu.make_async_copy(blocks, own_square, block_out).wait()


def kept_shapes():
    return [
        ((ROW, 3 * D), LOW), ((HEADS, ROW, ROW), LOW), ((ROW, 2 * HD), FULL), ((ROW, D), LOW), ((ROW, D), FULL)
    ]


def near_self(source_counts, target_counts, weights, gains, rows):
    total = rows.shape[0]
    tile = jnp.tile(gains.astype(LOW), (1, 4))
    lane_part = lax.broadcasted_iota(jnp.int32, tile.shape, 1) // UNIT
    tile = jnp.where(lane_part == lax.axis_index("dp") % 4, tile, jnp.zeros_like(tile))
    tile = jnp.pad(tile, ((0, 16 - tile.shape[0]), (0, 0)))
    dma = pltpu.SemaphoreType.DMA
    kept = kept_shapes()
    outs = [
        shape_of((2, BLOCKS, DEPTHS, SIDES, CORES, UNIT, D), LOW),
        shape_of((2, DEPTHS, SIDES, CORES, SLABS, UNIT, D), LOW),
        shape_of((SELFS, DEPTHS, SIDES, CORES, UNIT, D), LOW),
        shape_of((2, 8, D), FULL),
        shape_of((total // 2, ROW, D), LOW),
    ]
    square, tall, own_square, every_gain, away, *kept = pl.pallas_call(
        near_self_kernel,
        grid=(total,),
        in_specs=[SCALARS, SCALARS] + [constant(*value.shape) for value in weights] + [constant(16, 128), ANYWHERE],
        out_specs=[ANYWHERE] * 3
        + [pl.BlockSpec((2, 8, D), lambda row: (0, 0, 0)), ANYWHERE]
        + [per_row(*shape) for shape, _ in kept],
        out_shape=outs + [shape_of((total,) + shape, kind) for shape, kind in kept],
        scratch_shapes=[
            pltpu.VMEM((SELFS, DEPTHS, SIDES, CORES, UNIT, D), LOW),
            pltpu.VMEM((2, DEPTHS, SIDES, CORES, 16, 128), LOW),
            pltpu.VMEM((2, ROW, D), LOW),
            pltpu.VMEM((total // 2, ROW, D), LOW),
            pltpu.VMEM((ROW, ROW), FULL),
            pltpu.VMEM((UNITS, UNIT, D), LOW),
            dma((UNITS,)), dma((2,)), dma((SELFS, 5)), dma((SELFS, 5)), dma, dma((6,)), dma((6,)),
            dma((UNITS, 3)), dma((UNITS, 3)), dma((UNITS,)), dma((UNITS,)), dma((UNITS,)), dma((UNITS,)),
            dma((UNITS,)), dma((UNITS,)), dma((total // 2,)), dma((total // 2,)),
        ],
        compiler_params=pltpu.CompilerParams(
            vmem_limit_bytes=VMEM_LIMIT, collective_id=0, has_side_effects=True
        ),
        name="self_forward",
    )(source_counts, target_counts, *weights, tile, rows)
    return square.reshape(2, BLOCKS, D, D), tall.reshape(2, FF, D), own_square, every_gain, away, kept


def add_low(left, right):
    return (left.astype(FULL) + right.astype(FULL)).astype(LOW)


def near_back_kernel(
    kept_delta, sent_delta, rows, own_square, gains, triple, shares, inverse, result,
    square_sums, tall_sums, gain_sums,
    gradient, attention_in, attention_out, cross, expand, contract, gain_out,
    deltas, streams, value, delta_triple, sums, low_sums, own_gain,
    total, from_core, from_side, from_layer, middle, from_last, ending, from_depth,
    own_total, own_from_core, own_middle, own_from_side, own_from_depth,
    gain_total, gain_parts, gain_from_layer,
    delta_done, delta_sent, delta_arrived, fetched, stored,
    loaded, core_sent, core_done, first_sent, first_done, last_sent, last_done, depth_sent, depth_done,
    own_sent, own_done, gain_sent, gain_done,
):
    place = Place()
    layer, depth, side, core = place.layer, place.depth, place.side, place.core
    count = kept_delta.shape[0]
    step, steps_in_all = pl.program_id(0), 2 * count
    copies = Copies()

    def spot(which, unit, owner):
        if unit < BLOCKS:
            return square_sums.at[which, unit, :, :, owner]
        return tall_sums.at[which, :, :, owner, unit - BLOCKS]

    def load(unit, which):
        return pltpu.make_async_copy(spot(which, unit, core), total.at[unit, which], loaded.at[unit, which])

    def core_parts(unit, which):
        slot = (unit, which)
        return (
            spot(which, unit, 1 - core), from_core.at[slot], core_sent.at[slot], core_done.at[slot], place.sibling()
        )

    def first_parts(unit):
        if layer_first(unit):
            source, target, device = total.at[unit, :, :, 1 - side], from_side.at[unit], place.across_side()
        else:
            source, target, device = total.at[unit, 1 - layer], from_layer.at[unit], place.across_layer()
        return source, target, first_sent.at[unit], first_done.at[unit], device

    def last_parts(unit):
        if layer_first(unit):
            source, device = middle.at[unit, 1 - layer], place.across_layer()
        else:
            source, device = middle.at[unit, 1 - side], place.across_side()
        return source, from_last.at[unit], last_sent.at[unit], last_done.at[unit], device

    def deep_parts(unit, away_by):
        slot = (unit, away_by - 1)
        return (
            ending.at[unit, place.other_depth(away_by)], from_depth.at[slot], depth_sent.at[slot],
            depth_done.at[slot], place.along_depth(away_by),
        )

    def delta_parts(slot):
        return (
            sent_delta.at[slot], deltas.at[count + slot], delta_sent.at[slot], delta_arrived.at[slot],
            place.across_layer(),
        )

    def own_core_parts(unit):
        return (
            low_sums.at[unit, :, :, 1 - core], own_from_core.at[unit], own_sent.at[unit, 0], own_done.at[unit, 0],
            place.sibling(),
        )

    def own_side_parts(unit):
        return (
            own_total.at[unit, :, 1 - side], own_from_side.at[unit], own_sent.at[unit, 1], own_done.at[unit, 1],
            place.across_side(),
        )

    def own_deep_parts(unit, away_by):
        return (
            own_middle.at[unit, place.other_depth(away_by)], own_from_depth.at[unit, away_by - 1],
            own_sent.at[unit, 1 + away_by], own_done.at[unit, 1 + away_by], place.along_depth(away_by),
        )

    def gain_parts_of(stage):
        if stage == 0:
            source, target, device = gain_sums.at[1 - layer], gain_from_layer, place.across_layer()
        elif stage == 1:
            source, target, device = gain_total.at[0], gain_parts.at[0], place.sibling()
        elif stage == 2:
            source, target, device = gain_total.at[1], gain_parts.at[1], place.across_side()
        else:
            away_by = stage - 2
            source, target = gain_total.at[2, place.other_depth(away_by)], gain_parts.at[2, away_by]
            device = place.along_depth(away_by)
        return source, target, gain_sent.at[stage], gain_done.at[stage], device

    across = range(1, DEPTHS)
    for unit in range(UNITS):
        for which in range(2):
            copies.define(("core", unit, which), partial(core_parts, unit, which))
        copies.define(("first", unit), partial(first_parts, unit))
        copies.define(("last", unit), partial(last_parts, unit))
        for away_by in across:
            copies.define(("deep", unit, away_by), partial(deep_parts, unit, away_by))
    for slot in range(count):
        copies.define(("delta", slot), partial(delta_parts, slot))
    for unit in range(SELFS):
        copies.define(("own core", unit), partial(own_core_parts, unit))
        copies.define(("own side", unit), partial(own_side_parts, unit))
        for away_by in across:
            copies.define(("own deep", unit, away_by), partial(own_deep_parts, unit, away_by))
    for stage in range(3 + DEPTHS - 1):
        copies.define(("gain", stage), partial(gain_parts_of, stage))

    def begin(unit):
        for which in range(2):
            copies.start(("core", unit, which))
            load(unit, which).start()

    def cross_first(unit):
        for which in range(2):
            load(unit, which).wait()
            copies.arrived(("core", unit, which))

            def add(row, carry):
                total[unit, which, row] = add_low(total[unit, which, row], from_core[unit, which, row])
                return carry

            lax.fori_loop(0, DEPTHS, add, 0)
        copies.start(("first", unit))

    def cross_last(unit):
        copies.arrived(("first", unit))
        if layer_first(unit):

            def add(index, carry):
                which, row = index // DEPTHS, index % DEPTHS
                middle[unit, which, row] = add_low(total[unit, which, row, side], from_side[unit, which, row])
                return carry

        else:

            def add(index, carry):
                which, row = index // DEPTHS, index % DEPTHS
                middle[unit, which, row] = add_low(total[unit, layer, row, which], from_layer[unit, row, which])
                return carry

        lax.fori_loop(0, 2 * DEPTHS, add, 0)
        copies.start(("last", unit))

    def along_depth(unit):
        copies.arrived(("last", unit))
        kept = layer if layer_first(unit) else side
        ending[unit] = add_low(middle[unit, kept], from_last[unit])
        copies.start(*[("deep", unit, away_by) for away_by in range(1, DEPTHS)])

    def finish(unit):
        whole = ending[unit, depth].astype(FULL)
        for away_by in range(1, DEPTHS):
            copies.arrived(("deep", unit, away_by))
            whole = whole + from_depth[unit, away_by - 1].astype(FULL)
        if unit < EXPAND:
            cross[:, columns(unit - CROSS)] = whole
        elif unit < BLOCKS:
            expand[:, columns(unit - EXPAND)] = whole
        else:
            contract[columns(unit - BLOCKS, UNIT), :] = whole

    def steps():
        gap, ahead = SCATTER_GAP, SCATTER_AHEAD

        def one(number):
            if ahead <= number + ahead < UNITS:
                begin(ORDER[number + ahead])
            if number < UNITS:
                cross_first(ORDER[number])
            if 0 <= number - gap < UNITS:
                cross_last(ORDER[number - gap])
            if 0 <= number - 2 * gap < UNITS:
                along_depth(ORDER[number - 2 * gap])
            if 0 <= number - 3 * gap < UNITS:
                finish(ORDER[number - 3 * gap])

        return [partial(one, number) for number in range(UNITS + 3 * gap)]

    def fetch(index):
        slot = (index + count) % steps_in_all
        return pltpu.make_async_copy(
            rows.at[row_of(layer, slot, count)], streams.at[index % 2], fetched.at[index % 2]
        )

    def store(index):
        slot = (index + count) % steps_in_all
        return pltpu.make_async_copy(
            value.at[index % 2], gradient.at[row_of(layer, slot, count)], stored.at[index % 2]
        )

    take = pltpu.make_async_copy(kept_delta, deltas.at[pl.ds(0, count)], delta_done)

    @pl.when(step == 0)
    def _():
        take.start()
        fetch(step).start()
        sums[...] = jnp.zeros(sums.shape, FULL)
        own_gain[...] = jnp.zeros(own_gain.shape, FULL)
        place.greet()
        for number in range(SCATTER_AHEAD):
            begin(ORDER[number])
        copies.start(*[("delta", slot) for slot in range(count)])
        copies.start(("gain", 0))
        take.wait()

    for slot in range(count):

        @pl.when(step == count + slot)
        def _(slot=slot):
            copies.arrived(("delta", slot))

    plan = Plan(SCATTER_RATE, HOOKS)
    plan.fill(steps(), steps_in_all)

    @pl.when(step + 1 < steps_in_all)
    def _():
        fetch(step + 1).start()

    fetch(step).wait()
    delta, delta_gain = self_back(
        deltas[step], streams[step % 2].astype(FULL), gains[layer, 0:1, :],
        lambda unit: own_square[unit].reshape(D, D),
        triple.at[0], shares.at[0], inverse.at[0], result.at[0], delta_triple, sums, plan.hook,
    )
    own_gain[0:1, :] += delta_gain

    @pl.when(step >= 2)
    def _():
        store(step).wait()

    value[step % 2] = delta
    store(step).start()
    plan.hook()

    @pl.when(step == steps_in_all - 1)
    def _():
        for unit in range(SELFS):
            low_sums[unit] = sums[unit].astype(LOW).reshape(DEPTHS, SIDES, CORES, UNIT, D)
            copies.start(("own core", unit))
        copies.arrived(("gain", 0))
        whole = gain_sums[layer] + gain_from_layer[...] + own_gain[...]
        for row in range(DEPTHS):
            gain_total[0, row] = whole[:, 128 * row : 128 * (row + 1)]
        copies.start(("gain", 1))
        for unit in range(SELFS):
            copies.arrived(("own core", unit))

            def add(row, carry):
                own_total[unit, row] = add_low(low_sums[unit, row, :, core], own_from_core[unit, row])
                return carry

            lax.fori_loop(0, DEPTHS, add, 0)
            copies.start(("own side", unit))
        copies.arrived(("gain", 1))
        gain_total[1] = gain_total[0] + gain_parts[0]
        copies.start(("gain", 2))
        for unit in range(SELFS):
            copies.arrived(("own side", unit))
            own_middle[unit] = add_low(own_total[unit, :, side], own_from_side[unit])
            copies.start(*[("own deep", unit, away_by) for away_by in across])
        copies.arrived(("gain", 2))
        gain_total[2] = gain_total[1] + gain_parts[1]
        copies.start(*[("gain", 2 + away_by) for away_by in across])
        for unit in range(SELFS):
            whole = own_middle[unit, depth].astype(FULL)
            for away_by in range(1, DEPTHS):
                copies.arrived(("own deep", unit, away_by))
                whole = whole + own_from_depth[unit, away_by - 1].astype(FULL)
            if unit < OUT:
                attention_in[:, columns(unit)] = whole
            else:
                attention_out[...] = whole
        whole = gain_total[2, depth]
        for away_by in range(1, DEPTHS):
            copies.arrived(("gain", 2 + away_by))
            whole = whole + gain_parts[2, away_by]
        gain_out[...] = whole
        store(step - 1).wait()
        store(step).wait()
        copies.finish()


def near_back(kept_delta, sent_delta, rows, own_square, gains, kept, square_sums, tall_sums, gain_sums):
    count, total = kept_delta.shape[0], rows.shape[0]
    dma = pltpu.SemaphoreType.DMA
    vmem = pl.BlockSpec(memory_space=pltpu.VMEM)
    shapes = kept_shapes()[:4]

    def rotated(*shape):
        return pl.BlockSpec((1,) + shape, lambda step: ((step + count) % total,) + (0,) * len(shape))

    weight_shapes = [(UNIT, 3 * D), (UNIT, D), (UNIT, 2 * D), (UNIT, FF), (SLABS * UNIT, D), (8, 128)]
    low = lambda *shape: pltpu.VMEM(shape, LOW)
    full = lambda *shape: pltpu.VMEM(shape, FULL)
    gradient, *weights, gain = pl.pallas_call(
        near_back_kernel,
        grid=(total,),
        in_specs=[ANYWHERE, ANYWHERE, ANYWHERE, constant(SELFS, DEPTHS, SIDES, CORES, UNIT, D), constant(2, 8, D)]
        + [rotated(*shape) for shape, _ in shapes]
        + [ANYWHERE, ANYWHERE, constant(2, 8, D)],
        out_specs=[ANYWHERE] + [pl.BlockSpec(shape, lambda step: (0, 0)) for shape in weight_shapes],
        out_shape=[shape_of((total, ROW, D), FULL)] + [shape_of(shape, FULL) for shape in weight_shapes],
        scratch_shapes=[
            low(total, ROW, D), low(2, ROW, D), full(2, ROW, D), low(ROW, 3 * D), full(SELFS, D, D),
            low(SELFS, DEPTHS, SIDES, CORES, UNIT, D), full(8, D),
            low(UNITS, 2, DEPTHS, SIDES, UNIT, D), low(UNITS, 2, DEPTHS, SIDES, UNIT, D),
            low(UNITS, 2, DEPTHS, UNIT, D), low(UNITS, DEPTHS, 2, UNIT, D), low(UNITS, 2, DEPTHS, UNIT, D),
            low(UNITS, DEPTHS, UNIT, D), low(UNITS, DEPTHS, UNIT, D), low(UNITS, 3, UNIT, D),
            low(SELFS, DEPTHS, SIDES, UNIT, D), low(SELFS, DEPTHS, SIDES, UNIT, D),
            low(SELFS, DEPTHS, UNIT, D), low(SELFS, DEPTHS, UNIT, D), low(SELFS, 3, UNIT, D),
            full(3, DEPTHS, 8, 128), full(3, DEPTHS, 8, 128), full(8, D),
            dma, dma((count,)), dma((count,)), dma((2,)), dma((2,)),
            dma((UNITS, 2)), dma((UNITS, 2)), dma((UNITS, 2)), dma((UNITS,)), dma((UNITS,)), dma((UNITS,)),
            dma((UNITS,)), dma((UNITS, 3)), dma((UNITS, 3)),
            dma((SELFS, 5)), dma((SELFS, 5)), dma((6,)), dma((6,)),
        ],
        compiler_params=pltpu.CompilerParams(
            vmem_limit_bytes=VMEM_LIMIT, collective_id=1, has_side_effects=True
        ),
        name="self_back",
    )(
        kept_delta, sent_delta, rows, own_square, gains, *kept[:4],
        square_sums.reshape(2, BLOCKS, DEPTHS, SIDES, CORES, UNIT, D),
        tall_sums.reshape(2, DEPTHS, SIDES, CORES, SLABS, UNIT, D), gain_sums,
    )
    start = lax.axis_index("dp") % 4 * UNIT
    return gradient, *weights, lax.dynamic_slice_in_dim(gain[:3], start, UNIT, axis=1)


def far_self_kernel(
    source_counts, target_counts, rows, square, gains, triple, shares, inverse, result, first, bias
):
    layer, step, count = lax.axis_index("pipe"), pl.program_id(0), pl.num_programs(0) // 2
    row = row_of(layer, step, count)
    causal = layer == 1
    both = [jnp.where(causal, target_counts[row, piece], source_counts[row, piece]) for piece in range(PACK)]
    fill_bias(bias, *segments(both), causal)
    first[0] = self_forward(
        rows[0].astype(FULL), gains[layer, 0:1, :], lambda unit: square[unit], bias,
        triple.at[0], shares.at[0], inverse.at[0], result.at[0], no_hook,
    )


def far_self(source_counts, target_counts, square, gains, rows):
    total = rows.shape[0]
    kept = kept_shapes()
    return pl.pallas_call(
        far_self_kernel,
        grid=(total,),
        in_specs=[SCALARS, SCALARS, per_row(ROW, D), constant(SELFS, D, D), constant(2, 8, D)],
        out_specs=[per_row(*shape) for shape, _ in kept],
        out_shape=[shape_of((total,) + shape, kind) for shape, kind in kept],
        scratch_shapes=[pltpu.VMEM((ROW, ROW), FULL)],
        compiler_params=PARAMS,
        name="self_forward",
    )(source_counts, target_counts, rows, square, gains)


def far_back_kernel(
    deltas, rows, square, gains, triple, shares, inverse, result, gradient, sums, gain_out, delta_triple
):
    layer, step = lax.axis_index("pipe"), pl.program_id(0)

    @pl.when(step == 0)
    def _():
        sums[...] = jnp.zeros(sums.shape, FULL)
        gain_out[...] = jnp.zeros(gain_out.shape, FULL)

    delta, delta_gain = self_back(
        deltas[0], rows[0].astype(FULL), gains[layer, 0:1, :], lambda unit: square[unit],
        triple.at[0], shares.at[0], inverse.at[0], result.at[0], delta_triple, sums, no_hook,
    )
    gain_out[0:1, :] += delta_gain
    gradient[0] = delta


def far_back(deltas, rows, square, gains, kept):
    total = rows.shape[0]
    return pl.pallas_call(
        far_back_kernel,
        grid=(total,),
        in_specs=[per_row(ROW, D), per_row(ROW, D), constant(SELFS, D, D), constant(2, 8, D)]
        + [per_row(*shape) for shape, _ in kept_shapes()[:4]],
        out_specs=[per_row(ROW, D), constant(SELFS, D, D), constant(8, D)],
        out_shape=[shape_of((total, ROW, D), FULL), shape_of((SELFS, D, D), FULL), shape_of((8, D), FULL)],
        scratch_shapes=[pltpu.VMEM((ROW, 3 * D), LOW)],
        compiler_params=PARAMS,
        name="self_back",
    )(deltas, rows, square, gains, *kept[:4])


def spotsof(value):
    return [value[:, start : start + D] for start in range(0, value.shape[1], D)]


def gather_all(value, axes):
    return lax.all_gather(value, axes, axis=0, tiled=False)


def far_weights(weights, gains, shards):
    attention_in, attention_out, cross, expand, contract = (value.astype(LOW) for value in weights)
    both = ("pipe", "dp")
    own = jnp.stack(spotsof(attention_in) + [attention_out])
    own = jnp.swapaxes(gather_all(own, "dp"), 0, 1).reshape(SELFS, D, D)
    square = gather_all(jnp.stack(spotsof(cross) + spotsof(expand)), both)
    square = jnp.swapaxes(square.reshape(2, shards, BLOCKS, D // shards, D), 1, 2)
    tall = gather_all(contract, both)
    gains = gather_all(gains.astype(LOW), both).reshape(2, shards, 3, D // shards)
    gains = jnp.swapaxes(gains, 1, 2).reshape(2, 3, D).astype(FULL)
    return own, square.reshape(2, BLOCKS, D, D), tall.reshape(2, FF, D), jnp.pad(gains, ((0, 0), (0, 5), (0, 0)))


def scattered(value, axes):
    return lax.psum_scatter(value, axes, scatter_dimension=0, tiled=False).astype(FULL)


def far_sums(own, own_gain, square, tall, gains, section, shards):
    both = ("pipe", "dp")
    share = D // shards
    own = scattered(jnp.swapaxes(own.reshape(SELFS, shards, share, D), 0, 1), "dp")
    square = jnp.swapaxes(square.reshape(2, BLOCKS, shards, share, D), 1, 2)
    square = scattered(square.reshape(2 * shards, BLOCKS, share, D), both)
    tall = scattered(tall.reshape(2 * shards, FF // shards, D), both)
    gains = gains + jnp.where(jnp.arange(2)[:, None, None] == section, own_gain[None], 0.0)
    gains = jnp.swapaxes(gains[:, :3].reshape(2, 3, shards, share), 1, 2)
    gains = scattered(gains.reshape(2 * shards, 3, share), both)

    def joined(value, first, last):
        return jnp.concatenate([value[block] for block in range(first, last)], axis=1)

    return (
        joined(own, QKV, OUT), own[OUT], joined(square, CROSS, EXPAND), joined(square, EXPAND, BLOCKS), tall, gains
    )


def swap(value):
    return lax.ppermute(value, "pipe", [(0, 1), (1, 0)])


def local(
    section_input,
    attention_in,
    attention_out,
    cross_weights,
    expand,
    contract,
    norm_gains,
    source_lengths,
    target_lengths,
    cotangent,
):
    section = lax.axis_index("pipe")
    shards = lax.axis_size("dp")
    near = shards == DEPTHS * SIDES * CORES
    rows = section_input[0]
    count = rows.shape[0] // 2
    weights = tuple(value[0] for value in (attention_in, attention_out, cross_weights, expand, contract))
    if near:
        square, tall, own_square, gains, away, kept = near_self(
            source_lengths, target_lengths, weights, norm_gains[0], rows
        )
    else:
        turn = jnp.where(section == 0, count, 0)
        own_square, square, tall, gains = far_weights(weights, norm_gains[0], shards)
        slots = jnp.roll(rows, turn, axis=0)
        kept = far_self(source_lengths, target_lengths, own_square, gains, slots)
        away = swap(kept[-1][:count].astype(LOW))
    section_output, sent_output, kept_delta, sent_delta, square_sums, tall_sums, gain_sums = middle(
        source_lengths, target_lengths, kept[-1], away, cotangent, square, tall, gains
    )
    away_output = swap(sent_output)
    if near:
        gradient, *weight_sums = near_back(
            kept_delta, sent_delta, rows, own_square, gains, kept, square_sums, tall_sums, gain_sums
        )
    else:
        deltas = jnp.concatenate([swap(sent_delta), kept_delta], axis=0)
        gradient, own_sums, own_gain = far_back(deltas, slots, own_square, gains, kept)
        gradient = jnp.roll(gradient, -turn, axis=0)
        weight_sums = far_sums(own_sums, own_gain, square_sums, tall_sums, gain_sums, section, shards)
    section_output = lax.dynamic_update_slice_in_dim(
        section_output, away_output.astype(FULL), count * (1 - section), axis=0
    )
    return (section_output[None], gradient[None]) + tuple(value[None] for value in weight_sums)


def solution(mesh):
    in_specs = (
        P("pipe", "dp", None, None),
        P("pipe", "dp", None),
        P("pipe", "dp", None),
        P("pipe", "dp", None),
        P("pipe", "dp", None),
        P("pipe", "dp", None),
        P("pipe", None, "dp"),
        P("dp", None),
        P("dp", None),
        P("dp", None, None),
    )
    out_specs = (
        P("pipe", "dp", None, None),
        P("pipe", "dp", None, None),
        P("pipe", "dp", None),
        P("pipe", "dp", None),
        P("pipe", "dp", None),
        P("pipe", "dp", None),
        P("pipe", "dp", None),
        P("pipe", None, "dp"),
    )
    return jax.shard_map(local, mesh=mesh, in_specs=in_specs, out_specs=out_specs, check_vma=False)
```

time: 645 us -> 351 us (0.54)
  waiting for transfers between devices: 306 us -> 0.01 us
  Pallas kernels: 162 us -> 330 us
  blocking collectives: 80.9 us -> 0 us
  other arithmetic: 34.4 us -> 3.54 us
  local copies, waits for them, and re-layouts: 34.3 us -> 10.1 us
  between operations: 14.2 us -> 0.9 us
    reduce_scatter x2 -> x0, waiting for transfers between devices: 179 us -> none  [scatter_sums(): lax.psum_scatter(value, axes, scatter_dimension=0, tiled=False).astype(FULL)]
    pallas_call x3, Pallas kernels: 162 us -> 330 us  [the longest x1 124 us: near_back(): pl.pallas_call(near_back_kernel, grid=(total,), in_specs=[ANYWHERE, ANYWH...]
    all_gather x2 -> x0, waiting for transfers between devices: 92.8 us -> none  [the longest x1 53.9 us: gather_weights(): every_tall = lax.all_gather(tall, axes, axis=0, tiled=False)]
    all_gather x1 -> x0, blocking collectives: 40.9 us -> none  [gather_weights(): every_gain = lax.all_gather(gains.astype(LOW), axes, axis=0, tiled=False)]
    unnamed x1 -> x0, blocking collectives: 40 us -> none
    ppermute x3 -> x1, waiting for transfers between devices: 33.8 us -> 0.01 us  [swap(): return lax.ppermute(value, 'pipe', [(0, 1), (1, 0)])]
    reshape x3 -> x0, local copies, waits for them, and re-layouts: 10.3 us -> none  [the longest x1 10.2 us: gather_weights(): every_square = every_square.reshape(2, shards, BLOCKS, D // shards, D)]
    transpose x1 -> x0, local copies, waits for them, and re-layouts: 10.2 us -> none  [scatter_sums(): jnp.swapaxes(square.reshape(2, BLOCKS, shards, D // shards, D), 1, 2)]
  transfers between devices with their start and end apart: 7 -> 1, of which waited for: 6 -> 0; matrix products, arithmetic and copies ran while one was open for 9% -> 0% of each run, Pallas kernels for 0% -> 36%
where the time goes in v3:
time: 351 us; the launch traced here: 345 us
  Pallas kernels  330 us (94%)
  local copies, waits for them, and re-layouts  10.1 us (3%)
  other arithmetic  3.54 us (1%)
    pallas_call x1, Pallas kernels, near_back(): pl.pallas_call(near_back_kernel, grid=(total,), in_specs=[ANYWHERE, ANYWH...  124 us
    pallas_call x1, Pallas kernels, near_self(): pl.pallas_call(near_self_kernel, grid=(total,), in_specs=[SCALARS, SCALAR...  110 us
    pallas_call x1, Pallas kernels, middle(): pl.pallas_call(middle_kernel, grid=(count + 1,), in_specs=[SCALARS, SCALA...  95.2 us
    unnamed x18, local copies, waits for them, and re-layouts  8.68 us
  transfers between devices with their start and end apart: 1, of which 0 were waited for; matrix products, arithmetic and copies ran while one was open for 0% of the time, Pallas kernels for 36%

profile of v3, /device:TPU:0, one launch (start us, length us, event | category | flops | bytes accessed | tf_op | source)
XLA Modules:
  0.0 345.4 jit_solution(16678149921556982332)
XLA Ops:
  0.7 0.7 convert_element_type.13
  1.4 0.1 tile.10
  1.5 0.6 pad.4.gains
  2.1 109.8 %self_forward.1 = (bf16[2,6,4,2,2,32,512]{6,5,4,3,2,1,0:T(8,128)(2,1)}, bf16[2,4,2,2,4,32,512]{6,5,4,3,2,1,0:T(8,128)(2,1)}, bf16[4,4,2,2,32,512]{5,4,3,2,1,0:T(...) custom-call(s32[4,4]{1,0:T(4,128)} %source_counts.3, ...), custom_call_target="tpu_custom_call" | custom-call | tf_op jit(solution)/shard_map/self_forward/pallas_call | solution.py:738
  111.9 95.2 %middle.1 = (f32[4,512,512]{2,1,0:T(8,128)}, bf16[2,512,512]{2,1,0:T(8,128)(2,1)}, bf16[2,512,512]{2,1,0:T(8,128)(2,1)}, bf16[2,512,512]{2,1,0:T(8,128)(2,1)}, b...) custom-call(s32[4,4]{1,0:T(4,128)} %source_counts.3, s32[4,4]{1,0:T(4,128)} %target_counts.3, ...), custom_call_target="tpu_custom_call" | custom-call | tf_op jit(solution)/shard_map/middle/pallas_call | solution.py:383
  207.1 1.3 collective-permute-start
  208.5 124.5 %self_back.1 = (f32[4,512,512]{2,1,0:T(8,128)}, f32[32,1536]{1,0:T(8,128)}, f32[32,512]{1,0:T(8,128)}, f32[32,1024]{1,0:T(8,128)}, f32[32,2048]{1,0:T(8,128)}, /*index=5*/f32[128,512]{1,0:T(8,128)}, f32[8,128]{1,0:T(8,128)}) custom-call(bf16[2,512,512]{2,1,0:T(8,128)(2,1)} %get-tuple-element.39.kept_delta, ...), custom_call_target="tpu_custom_call" | custom-call | tf_op jit(solution)/shard_map/self_back/pallas_call | solution.py:1064
  332.9 0.7 slice.3
  333.6 0.1 dynamic-slice_bitcast_fusion
  333.7 0.6 copy.18
  334.3 0.0 collective-permute-done
  334.3 2.8 convert_dynamic-update-slice_fusion
  337.1 0.0 copy-start.2
  337.1 0.0 copy-start.4
  337.1 0.0 copy-start.3
  337.1 0.0 copy-start.1
  337.1 0.0 copy-start
  337.1 4.7 %copy.29 = f32[1,4,512,512]{3,2,1,0:T(8,128)} copy(f32[1,4,512,512]{3,2,1,0:T(8,128)} %bitcast.30) | data formatting | bytes 8388608
  341.8 0.0 copy-done.2
  341.8 0.7 copy.30
  342.5 0.0 copy-done.4
  342.5 0.6 copy.31
  343.1 0.0 copy-done.3
  343.1 0.7 copy.32
  343.8 0.0 copy-done.1
  343.8 0.7 copy.33
  344.5 0.0 copy-done
  344.5 0.7 copy.34
  (5 shorter events, 0.0 us)
Async XLA Ops:
  207.1 127.1 %collective-permute-start = (bf16[2,512,512]{2,1,0:T(8,128)(2,1)}, bf16[2,512,512]{2,1,0:T(8,128)(2,1)}, u32[]{:S(2)}, u32[]{:S(2)}) collective-permute-start(bf16[2,512,512]{2,1,0:T(8,128)(2,1)} %get-tuple-element.38), channel_id=1, source_target_pairs={{0,16},{16,0},{1,17},{17,1},{2,18},{18,2},{3,19},{19,3},{4,20},{20... | collective-permute-start | bytes 3145736 | tf_op jit(solution)/shard_map/ppermute | solution.py:1206
  337.1 4.7 %copy-start.2 = (f32[32,1536]{1,0:T(8,128)S(1)}, f32[32,1536]{1,0:T(8,128)}, u32[]{:S(2)}) copy-start(f32[32,1536]{1,0:T(8,128)} %get-tuple-element.50) | copy-start | bytes 589828
  337.1 5.4 %copy-start.4 = (f32[32,512]{1,0:T(8,128)S(1)}, f32[32,512]{1,0:T(8,128)}, u32[]{:S(2)}) copy-start(f32[32,512]{1,0:T(8,128)} %get-tuple-element.51) | copy-start | bytes 196612
  337.1 6.1 %copy-start.3 = (f32[32,1024]{1,0:T(8,128)S(1)}, f32[32,1024]{1,0:T(8,128)}, u32[]{:S(2)}) copy-start(f32[32,1024]{1,0:T(8,128)} %get-tuple-element.52) | copy-start | bytes 393220
  337.1 6.7 %copy-start.1 = (f32[32,2048]{1,0:T(8,128)S(1)}, f32[32,2048]{1,0:T(8,128)}, u32[]{:S(2)}) copy-start(f32[32,2048]{1,0:T(8,128)} %get-tuple-element.53) | copy-start | bytes 786436
  337.1 7.4 %copy-start = (f32[128,512]{1,0:T(8,128)S(1)}, f32[128,512]{1,0:T(8,128)}, u32[]{:S(2)}) copy-start(f32[128,512]{1,0:T(8,128)} %get-tuple-element.54) | copy-start | bytes 786436
